TPU v7x, 32 devices: a whole 2x2x4 slice. The times are simulated.
32 devices in a mesh: seq: 16 (over z, y, x), head: 2 (over core).
Axes of the slice: x: 2, y: 2, z: 4, core: 2. Of those that a mesh axis runs over, the one named last changes fastest.
Arguments:
- layer_input: bfloat16 [8192, 2048], P('seq'), may hold values from -6 to 6
- seq_lengths: int32 [4], replicated, may hold values from 1 to 7936, as said below
- gain_attn: bfloat16 [2048], P('seq'), may hold values from 0.5 to 1.5
- w_query: bfloat16 [2048, 256], P('seq', 'head'), may hold values from -0.125 to 0.125
- w_key: bfloat16 [2048, 256], P('seq', 'head'), may hold values from -0.125 to 0.125
- w_value: bfloat16 [2048, 2048], P('seq', 'head'), may hold values from -0.125 to 0.125
- w_out: bfloat16 [2048, 2048], P('head', 'seq'), may hold values from -1 to 1
- gain_mlp: bfloat16 [2048], P('seq'), may hold values from 0.5 to 1.5
- w_gate: bfloat16 [2048, 5632], P('seq', 'head'), may hold values from -0.125 to 0.125
- w_up: bfloat16 [2048, 5632], P('seq', 'head'), may hold values from -0.125 to 0.125
- w_down: bfloat16 [5632, 2048], P('head', 'seq'), may hold values from -0.078125 to 0.078125
- cotangent: bfloat16 [8192, 2048], P('seq'), may hold values from -6 to 6
Outputs:
- layer_out: bfloat16 [8192, 2048], P('seq')
- input_grad: float32 [8192, 2048], P('seq')
- gain_attn_grad: float32 [2048], P('seq')
- w_query_grad: float32 [2048, 256], P('seq', 'head')
- w_key_grad: float32 [2048, 256], P('seq', 'head')
- w_value_grad: float32 [2048, 2048], P('seq', 'head')
- w_out_grad: float32 [2048, 2048], P('head', 'seq')
- gain_mlp_grad: float32 [2048], P('seq')
- w_gate_grad: float32 [2048, 5632], P('seq', 'head')
- w_up_grad: float32 [2048, 5632], P('seq', 'head')
- w_down_grad: float32 [5632, 2048], P('head', 'seq')
- den_stats: float32 [2], replicated
Inputs may be any that keep to these rules, and one draw needn't show every extreme that they name: `seq_lengths`: the sequences fill all 8192 positions; the longest has exactly 7936 positions.
All inputs are finite; a program needn't handle non-finite values.
Results may differ from a plain program's by a relative error of at most 0.012.
Values may be sent and summed in bfloat16 or wider, within the bound.
A program may use at most 256 MiB of HBM per device.

v0:
```python
import math

import jax
import jax.numpy as jnp
from jax import lax
from jax.sharding import PartitionSpec as P

H = 16
FD = 16
DV = 128


HIGH = lax.Precision.HIGHEST


def entering(value, axis, combine, identity, reverse):
    peers, index = (lax.axis_size(axis), lax.axis_index(axis))
    everything = jax.tree.map(lambda part: lax.all_gather(part, axis), value)
    start = jax.tree.map(
        lambda part, zero: jnp.broadcast_to(jnp.asarray(zero, part.dtype), part.shape),
        value,
        identity,
    )

    def hop(k, before):
        at = peers - 1 - k if reverse else k
        reached = at > index if reverse else at < index
        new = combine(before, jax.tree.map(lambda part: part[at], everything))
        return jax.tree.map(lambda a, b: jnp.where(reached, a, b), new, before)

    return lax.fori_loop(0, peers, hop, start)


def features(vectors):
    feat_width = vectors.shape[-1]
    outer_prod = (vectors[..., :, None] * vectors[..., None, :]).reshape(
        vectors.shape[:-1] + (feat_width * feat_width,)
    )
    ones_col = jnp.ones(vectors.shape[:-1] + (1,), vectors.dtype)
    return jnp.concatenate(
        [
            ones_col,
            vectors * feat_width ** (-0.25),
            outer_prod * (feat_width ** (-0.5) / math.sqrt(2.0)),
        ],
        axis=-1,
    )


def segment_starts(seq_lengths, positions):
    seq_starts = jnp.cumsum(seq_lengths) - seq_lengths
    picked = jnp.where(seq_starts[None, :] <= positions[:, None], seq_starts[None, :], 0)
    return jnp.max(picked, axis=1)


def link_states(earlier, later):
    keep_prev = 1.0 - later[2]
    return (
        later[0] + keep_prev * earlier[0],
        later[1] + keep_prev * earlier[1],
        jnp.maximum(earlier[2], later[2]),
    )


def rms_back(grad_normed, x_hat, inv_rms, gain_vec):
    grad_hat = grad_normed * gain_vec
    return inv_rms * (grad_hat - x_hat * jnp.mean(grad_hat * x_hat, axis=-1, keepdims=True))


def shards(
    layer_input,
    seq_lengths,
    gain_attn,
    w_query,
    w_key,
    w_value,
    w_out,
    gain_mlp,
    w_gate,
    w_up,
    w_down,
    cotangent,
):
    num_rows = layer_input.shape[0]
    block_first = lax.axis_index("seq") * num_rows
    positions = block_first + jnp.arange(num_rows, dtype=jnp.int32)
    seg_start = segment_starts(seq_lengths, positions)
    carried = (seg_start < block_first).astype(jnp.float32)
    tail_mask = (seg_start == seg_start[-1]).astype(jnp.float32)
    reset_flag = (seg_start[-1] >= block_first).astype(jnp.float32)
    local_pos = jnp.arange(num_rows)
    causal = (local_pos[None, :] <= local_pos[:, None]) & (seg_start[None, :] == seg_start[:, None])
    heads_here = H // lax.axis_size("head")
    scale_root = FD**0.5

    def core(query_f, key_f, value_f, state_in, norm_in):
        scores = jnp.einsum("thd,uhd->htu", query_f, key_f, precision=HIGH) / scale_root
        weights = jnp.where(causal[None], 1.0 + scores + 0.5 * scores * scores, 0.0)
        query_feat = features(query_f) * carried[:, None, None]
        numer = jnp.einsum("htu,uhv->thv", weights, value_f, precision=HIGH)
        numer = numer + jnp.einsum("thf,hfv->thv", query_feat, state_in, precision=HIGH)
        denom = jnp.sum(weights, axis=-1).T + jnp.einsum(
            "thf,hf->th", query_feat, norm_in, precision=HIGH
        )
        return (numer / denom[..., None], denom)

    def summary(key_f, value_f):
        key_feat = features(key_f) * tail_mask[:, None, None]
        return (
            jnp.einsum("thf,thv->hfv", key_feat, value_f, precision=HIGH),
            jnp.sum(key_feat, axis=0),
        )

    query_full, key_full, value_full, out_full, gain_one = (
        lax.all_gather(w_query, "seq", axis=0, tiled=True),
        lax.all_gather(w_key, "seq", axis=0, tiled=True),
        lax.all_gather(w_value, "seq", axis=0, tiled=True),
        lax.all_gather(w_out, "seq", axis=1, tiled=True),
        lax.all_gather(gain_attn, "seq", axis=0, tiled=True),
    )
    x_float = layer_input.astype(jnp.float32)
    inv_rms_one = lax.rsqrt(jnp.mean(x_float * x_float, axis=-1, keepdims=True) + 1e-05)
    x_hat_one = x_float * inv_rms_one
    gain_one_f = gain_one.astype(jnp.float32)
    normed_attn = (x_hat_one * gain_one_f).astype(jnp.bfloat16)
    query = jnp.dot(normed_attn, query_full, preferred_element_type=jnp.float32).astype(
        jnp.bfloat16
    )
    key_rows = jnp.dot(normed_attn, key_full, preferred_element_type=jnp.float32).astype(
        jnp.bfloat16
    )
    value_rows = jnp.dot(normed_attn, value_full, preferred_element_type=jnp.float32).astype(
        jnp.bfloat16
    )
    query_f = query.astype(jnp.float32).reshape(num_rows, heads_here, FD)
    key_f = key_rows.astype(jnp.float32).reshape(num_rows, heads_here, FD)
    value_f = value_rows.astype(jnp.float32).reshape(num_rows, heads_here, DV)
    state_out, norm_out = summary(key_f, value_f)
    state_in, norm_in, _ = entering(
        (state_out, norm_out, reset_flag),
        "seq",
        link_states,
        (jnp.zeros_like(state_out), jnp.zeros_like(norm_out), jnp.zeros((), jnp.float32)),
        False,
    )
    mixed, denom = core(query_f, key_f, value_f, state_in, norm_in)
    mixed_low = mixed.reshape(num_rows, heads_here * DV).astype(jnp.bfloat16)
    attn_branch = lax.psum(jnp.dot(mixed_low, out_full, preferred_element_type=jnp.float32), "head")
    resid = x_float + attn_branch
    gate_full, up_full, down_full, gain_two = (
        lax.all_gather(w_gate, "seq", axis=0, tiled=True),
        lax.all_gather(w_up, "seq", axis=0, tiled=True),
        lax.all_gather(w_down, "seq", axis=1, tiled=True),
        lax.all_gather(gain_mlp, "seq", axis=0, tiled=True),
    )
    inv_rms_two = lax.rsqrt(jnp.mean(resid * resid, axis=-1, keepdims=True) + 1e-05)
    x_hat_two = resid * inv_rms_two
    gain_two_f = gain_two.astype(jnp.float32)
    normed_mlp = (x_hat_two * gain_two_f).astype(jnp.bfloat16)
    gate = jnp.dot(normed_mlp, gate_full, preferred_element_type=jnp.float32)
    up_proj = jnp.dot(normed_mlp, up_full, preferred_element_type=jnp.float32)
    sigma = jax.nn.sigmoid(gate)
    silu_gate = gate * sigma
    hidden = (silu_gate * up_proj).astype(jnp.bfloat16)
    mlp_branch = lax.psum(
        jnp.dot(hidden, down_full, preferred_element_type=jnp.float32).astype(jnp.bfloat16), "head"
    ).astype(jnp.float32)
    layer_out = (resid + mlp_branch).astype(jnp.bfloat16)
    neg_least, largest = lax.pmax((-jnp.min(denom), jnp.max(denom)), ("seq", "head"))
    den_stats = jnp.stack([jnp.log(-neg_least), jnp.log(largest)])
    gate_back, up_back, down_back, gain_two_back = (
        lax.all_gather(w_gate, "seq", axis=0, tiled=True),
        lax.all_gather(w_up, "seq", axis=0, tiled=True),
        lax.all_gather(w_down, "seq", axis=1, tiled=True),
        lax.all_gather(gain_mlp, "seq", axis=0, tiled=True),
    )
    grad_out = cotangent.astype(jnp.float32)
    down_grad = jnp.dot(hidden.T, cotangent, preferred_element_type=jnp.float32)
    grad_hidden = jnp.dot(cotangent, down_back.T, preferred_element_type=jnp.float32)
    grad_gate = (grad_hidden * up_proj * sigma * (1.0 + gate * (1.0 - sigma))).astype(jnp.bfloat16)
    grad_up = (grad_hidden * silu_gate).astype(jnp.bfloat16)
    gate_grad = jnp.dot(normed_mlp.T, grad_gate, preferred_element_type=jnp.float32)
    up_grad = jnp.dot(normed_mlp.T, grad_up, preferred_element_type=jnp.float32)
    grad_normed_part = jnp.dot(
        grad_gate, gate_back.T, preferred_element_type=jnp.float32
    ) + jnp.dot(grad_up, up_back.T, preferred_element_type=jnp.float32)
    grad_normed_mlp = lax.psum(grad_normed_part, "head")
    gain_two_grad = jnp.sum(grad_normed_mlp * x_hat_two, axis=0)
    grad_resid = grad_out + rms_back(
        grad_normed_mlp, x_hat_two, inv_rms_two, gain_two_back.astype(jnp.float32)
    )
    gate_grad, up_grad, down_grad, gain_two_grad = (
        lax.psum_scatter(gate_grad, "seq", scatter_dimension=0, tiled=True),
        lax.psum_scatter(up_grad, "seq", scatter_dimension=0, tiled=True),
        lax.psum_scatter(down_grad, "seq", scatter_dimension=1, tiled=True),
        lax.psum_scatter(gain_two_grad, "seq", scatter_dimension=0, tiled=True),
    )
    query_back, key_back, value_back, out_back, gain_one_back = (
        lax.all_gather(w_query, "seq", axis=0, tiled=True),
        lax.all_gather(w_key, "seq", axis=0, tiled=True),
        lax.all_gather(w_value, "seq", axis=0, tiled=True),
        lax.all_gather(w_out, "seq", axis=1, tiled=True),
        lax.all_gather(gain_attn, "seq", axis=0, tiled=True),
    )
    grad_attn = grad_resid.astype(jnp.bfloat16)
    out_grad = jnp.dot(mixed_low.T, grad_attn, preferred_element_type=jnp.float32)
    grad_mixed = jnp.dot(grad_attn, out_back.T, preferred_element_type=jnp.float32).reshape(
        num_rows, heads_here, DV
    )
    _, core_pull, _ = jax.vjp(core, query_f, key_f, value_f, state_in, norm_in, has_aux=True)
    grad_query_f, grad_key_f, grad_value_f, grad_state_in, grad_norm_in = core_pull(grad_mixed)
    grad_state_out, grad_norm_out, _ = entering(
        (grad_state_in, grad_norm_in, reset_flag),
        "seq",
        link_states,
        (jnp.zeros_like(grad_state_in), jnp.zeros_like(grad_norm_in), jnp.zeros((), jnp.float32)),
        True,
    )
    _, summary_pull = jax.vjp(summary, key_f, value_f)
    key_more, value_more = summary_pull((grad_state_out, grad_norm_out))
    grad_query = grad_query_f.reshape(num_rows, heads_here * FD).astype(jnp.bfloat16)
    grad_key = (grad_key_f + key_more).reshape(num_rows, heads_here * FD).astype(jnp.bfloat16)
    grad_value = (grad_value_f + value_more).reshape(num_rows, heads_here * DV).astype(jnp.bfloat16)
    query_grad = jnp.dot(normed_attn.T, grad_query, preferred_element_type=jnp.float32)
    key_grad = jnp.dot(normed_attn.T, grad_key, preferred_element_type=jnp.float32)
    value_grad = jnp.dot(normed_attn.T, grad_value, preferred_element_type=jnp.float32)
    grad_attn_part = (
        jnp.dot(grad_query, query_back.T, preferred_element_type=jnp.float32)
        + jnp.dot(grad_key, key_back.T, preferred_element_type=jnp.float32)
        + jnp.dot(grad_value, value_back.T, preferred_element_type=jnp.float32)
    )
    grad_normed_attn = lax.psum(grad_attn_part, "head")
    gain_one_grad = jnp.sum(grad_normed_attn * x_hat_one, axis=0)
    input_grad = grad_resid + rms_back(
        grad_normed_attn, x_hat_one, inv_rms_one, gain_one_back.astype(jnp.float32)
    )
    query_grad, key_grad, value_grad, out_grad, gain_one_grad = (
        lax.psum_scatter(query_grad, "seq", scatter_dimension=0, tiled=True),
        lax.psum_scatter(key_grad, "seq", scatter_dimension=0, tiled=True),
        lax.psum_scatter(value_grad, "seq", scatter_dimension=0, tiled=True),
        lax.psum_scatter(out_grad, "seq", scatter_dimension=1, tiled=True),
        lax.psum_scatter(gain_one_grad, "seq", scatter_dimension=0, tiled=True),
    )
    return (
        layer_out,
        input_grad,
        gain_one_grad,
        query_grad,
        key_grad,
        value_grad,
        out_grad,
        gain_two_grad,
        gate_grad,
        up_grad,
        down_grad,
        den_stats,
    )


def solution(mesh):
    return jax.shard_map(
        shards,
        mesh=mesh,
        in_specs=(
            P("seq", None),
            P(),
            P("seq"),
            P("seq", "head"),
            P("seq", "head"),
            P("seq", "head"),
            P("head", "seq"),
            P("seq"),
            P("seq", "head"),
            P("seq", "head"),
            P("head", "seq"),
            P("seq", None),
        ),
        out_specs=(
            P("seq", None),
            P("seq", None),
            P("seq"),
            P("seq", "head"),
            P("seq", "head"),
            P("seq", "head"),
            P("head", "seq"),
            P("seq"),
            P("seq", "head"),
            P("seq", "head"),
            P("head", "seq"),
            P(),
        ),
        check_vma=False,
    )
```

profile of v0, /device:TPU:0, one launch (start us, length us, event | category | flops | bytes accessed | tf_op | source)
XLA Modules:
  0.0 3665.2 jit_solution(560621732810649776)
XLA Ops:
  10.1 42.4 %all-gather.4 = bf16[16,1,128]{2,1,0:T(2,128)(2,1)S(1)} all-gather(bf16[1,1,128]{2,1,0:T(2,128)(2,1)} %bitcast.232), channel_id=1, replica_groups=mesh['seq'=16,'head'=2] {'seq'}, dimensions={0}, use_global_device_ids=true | all-gather | bytes 4352 | tf_op jit(solution)/shard_map/all_gather | solution.py:119
  55.3 42.2 %all_gather.74 = bf16[2048,128]{1,0:T(8,128)(2,1)S(1)} all-gather(bf16[128,128]{1,0:T(8,128)(2,1)} %param.20), channel_id=1, replica_groups=mesh['seq'=16,'head'=2] {'seq'}, dimensions={0}, use_global_device_ids=true | all-gather | bytes 557056 | tf_op jit(solution)/shard_map/all_gather | solution.py:116
  104.1 4.7 fusion.30
  118.4 56.0 %all-gather.1 = f32[128,273]{1,0:T(8,128)} all-gather(f32[8,273]{1,0:T(8,128)S(1)} %fusion.65), channel_id=3, replica_groups=mesh['seq'=16,'head'=2] {'seq'}, dimensions={0}, use_global_device_ids=true | all-gather | bytes 148512 | tf_op jit(solution)/shard_map/all_gather | solution.py:18
  175.8 58.4 %all-reduce = f32[16]{0:T(128)S(1)} all-reduce(f32[16]{0:T(128)S(1)} %dynamic-update-slice), channel_id=1, replica_groups=mesh['seq'=16,'head'=2] {'seq'}, use_global_device_ids=true, to_apply=%add | all-reduce | flops 16 | bytes 128
  234.2 59.0 %all_gather.73 = bf16[2048,128]{1,0:T(8,128)(2,1)S(1)} all-gather(bf16[128,128]{1,0:T(8,128)(2,1)S(1)} %copy-done.48), channel_id=1, replica_groups=mesh['seq'=16,'head'=2] {'seq'}, dimensions={0}, use_global_device_ids=true | all-gather | bytes 557056 | tf_op jit(solution)/shard_map/all_gather | solution.py:115
  303.0 6.6 fusion.22
  309.6 186.0 %all-gather.24.cloned.1.call-done = f32[128,273,128]{2,0,1:T(8,128)} async-done(((f32[8,273,128]{2,0,1:T(8,128)}), f32[128,273,128]{2,0,1:T(8,128)}) %all-gather.24.cloned.1.call-update) | async-done | bytes 17891344 | tf_op jit(solution)/shard_map/all_gather | solution.py:18
  495.6 62.3 %while.34 = (s32[]{:T(128)}, f32[8,273,128]{2,1,0:T(8,128)S(1)}, f32[8,273]{1,0:T(8,128)S(1)}, s32[]{:T(128)}, f32[16,8,273,128]{3,1,0,2:T(8,128)}, /*index=5*/f...) while((s32[]{:T(128)}, f32[8,273,128]{2,1,0:T(8,128)S(1)}, ...), condition=%wide.region_5.6_spmd.clone, body=%wide.region_4.5_spmd.clone.sunk | while | flops 1126949 | bytes 5617411 | solution.py:31
  557.9 5.4 fusion.55
  564.0 7.5 fusion.28
  571.5 17.1 all-gather.16.cloned.1.call-done
  588.6 6.5 fusion.68
  597.1 37.6 %all-gather.5 = bf16[16,1,128]{2,1,0:T(2,128)(2,1)S(1)} all-gather(bf16[1,1,128]{2,1,0:T(2,128)(2,1)S(1)} %bitcast.233), channel_id=1, replica_groups=mesh['seq'=16,'head'=2] {'seq'}, dimensions={0}, use_global_device_ids=true | all-gather | bytes 4352 | tf_op jit(solution)/shard_map/all_gather | solution.py:154
  640.3 128.0 %all-gather.18.cloned.1.call-done = bf16[2048,2816]{1,0:T(8,128)(2,1)} async-done(((bf16[128,2816]{1,0:T(8,128)(2,1)}), bf16[2048,2816]{1,0:T(8,128)(2,1)}) %all-gather.18.cloned.1.call-update) | async-done | bytes 11534352 | tf_op jit(solution)/shard_map/all_gather | solution.py:151
  768.3 11.1 fusion.69
  779.4 132.3 %all-gather.20.cloned.1.call-done = bf16[2048,2816]{1,0:T(8,128)(2,1)} async-done(((bf16[128,2816]{1,0:T(8,128)(2,1)}), bf16[2048,2816]{1,0:T(8,128)(2,1)}) %all-gather.20.cloned.1.call-update) | async-done | bytes 11534352 | tf_op jit(solution)/shard_map/all_gather | solution.py:152
  911.7 12.6 fusion.70
  924.2 171.3 %all-gather.22.cloned.1.call-done = bf16[2816,2048]{1,0:T(8,128)(2,1)} async-done(((bf16[2816,128]{1,0:T(8,128)(2,1)}), bf16[2816,2048]{1,0:T(8,128)(2,1)}) %all-gather.22.cloned.1.call-update) | async-done | bytes 11534352 | tf_op jit(solution)/shard_map/all_gather | solution.py:153
  1095.5 15.8 multiply_convert_fusion
  1111.3 10.9 fusion.71
  1122.2 10.6 convolution_add_fusion
  1132.9 10.9 convolution_convert_fusion
  1144.5 15.1 all-reduce.14.cloned.1.call-done
  1164.6 20.3 all-reduce.12.cloned.1.call-done
  1185.0 6.1 multiply_add_fusion.1
  1194.8 4.8 fusion.24
  1200.9 6.1 fusion.53
  1207.0 59.3 %all-gather.3 = f32[128,273]{1,0:T(8,128)} all-gather(f32[8,273]{1,0:T(8,128)S(1)} %bitcast.231), channel_id=5, replica_groups=mesh['seq'=16,'head'=2] {'seq'}, dimensions={0}, use_global_device_ids=true | all-gather | bytes 148512 | tf_op jit(solution)/shard_map/all_gather | solution.py:18
  1274.9 11.0 fusion.7
  1292.0 11.3 fusion.20
  1303.3 272.1 %all-gather.26.cloned.1.call-done = f32[128,273,128]{2,0,1:T(8,128)} async-done(((f32[8,273,128]{2,0,1:T(8,128)}), f32[128,273,128]{2,0,1:T(8,128)}) %all-gather.26.cloned.1.call-update) | async-done | bytes 17891344 | tf_op jit(solution)/shard_map/all_gather | solution.py:18
  1575.5 62.5 %while.35 = (s32[]{:T(128)}, f32[8,273,128]{2,1,0:T(8,128)S(1)}, f32[8,273]{1,0:T(8,128)S(1)}, s32[]{:T(128)}, f32[16,8,273,128]{3,1,0,2:T(8,128)}, /*index=5*/f...) while((s32[]{:T(128)}, f32[8,273,128]{2,1,0:T(8,128)S(1)}, ...), condition=%wide.region_16.17_spmd.clone, body=%wide.region_15.16_spmd.clone.sunk | while | flops 1126953 | bytes 5617473 | solution.py:31
  1645.2 4.6 add_convert_fusion.1
  1662.6 8.5 fusion.40
  1672.9 14.8 fusion.77
  1687.8 13.3 fusion.78
  1701.1 13.2 fusion.79
  1715.6 5.8 fusion.76
  1722.8 40.6 %all-reduce.3 = (f32[]{:T(128)}, f32[]{:T(128)}) all-reduce(f32[]{:T(128)} %get-tuple-element.403, f32[]{:T(128)S(6)} %neg.22), channel_id=1, replica_groups=mesh['seq'=16,'head'=2] {'seq','head'}, use_global_device_ids=true, to_apply=%region_35.36 | all-reduce | flops 2 | bytes 16 | tf_op jit(solution)/shard_map/pmax | solution.py:169
  1768.7 80.9 %all-reduce.4 = (f32[2048]{0:T(1024)S(1)}, f32[2048]{0:T(1024)S(1)}) all-reduce(f32[2048]{0:T(1024)S(1)} %get-tuple-element.396, f32[2048]{0:T(1024)S(1)} %get-tuple-element.394), channel_id=6, replica_groups=mesh['seq'=16,'head'=2] {'seq'}, use_global_device_ids=true, to_apply=%region_22.23.clone | all-reduce | flops 4096 | bytes 32768
  1850.8 6.6 fusion.17
  1857.4 93.0 %reduce-scatter.14.cloned.1.call-done = f32[1024,128]{1,0:T(8,128)} async-done(((f32[1024,2048]{1,0:T(8,128)}), f32[1024,128]{1,0:T(8,128)}) %reduce-scatter.14.cloned.1.call-update) | async-done | bytes 524304 | tf_op jit(solution)/shard_map/reduce_scatter | solution.py:241
  1950.4 82.9 %reduce-scatter.10.cloned.1.call-done = f32[128,128]{1,0:T(8,128)} async-done(((f32[2048,128]{1,0:T(8,128)}), f32[128,128]{1,0:T(8,128)}) %reduce-scatter.10.cloned.1.call-update) | async-done | bytes 65552 | tf_op jit(solution)/shard_map/reduce_scatter | solution.py:239
  2033.4 472.1 %reduce-scatter.16.cloned.1.call-done = f32[128,2816]{1,0:T(8,128)} async-done(((f32[2048,2816]{1,0:T(8,128)}), f32[128,2816]{1,0:T(8,128)}) %reduce-scatter.16.cloned.1.call-update) | async-done | bytes 1441808 | tf_op jit(solution)/shard_map/reduce_scatter | solution.py:193
  2505.5 482.5 %reduce-scatter.18.cloned.1.call-done = f32[128,2816]{1,0:T(8,128)} async-done(((f32[2048,2816]{1,0:T(8,128)}), f32[128,2816]{1,0:T(8,128)}) %reduce-scatter.18.cloned.1.call-update) | async-done | bytes 1441808 | tf_op jit(solution)/shard_map/reduce_scatter | solution.py:194
  2988.0 482.6 %reduce-scatter.20.cloned.1.call-done = f32[2816,128]{1,0:T(8,128)} async-done(((f32[2816,2048]{1,0:T(8,128)}), f32[2816,128]{1,0:T(8,128)}) %reduce-scatter.20.cloned.1.call-update) | async-done | bytes 1441808 | tf_op jit(solution)/shard_map/reduce_scatter | solution.py:195
  3470.6 187.4 %reduce-scatter.12.cloned.1.call-done = f32[128,1024]{1,0:T(8,128)} async-done(((f32[2048,1024]{1,0:T(8,128)}), f32[128,1024]{1,0:T(8,128)}) %reduce-scatter.12.cloned.1.call-update) | async-done | bytes 524304 | tf_op jit(solution)/shard_map/reduce_scatter | solution.py:240
  (367 shorter events, 196.8 us)
Async XLA Ops:
  7.2 97.0 %all-gather.14.cloned.1.call-start = ((), (), s32[]{:S(2)}) async-start(), calls=%async_computation.7 | async-start | bytes 4456448 | tf_op jit(solution)/shard_map/all_gather | solution.py:117
  7.9 487.6 %all-gather.24.cloned.1.call-start = ((), (), s32[]{:S(2)}) async-start(), calls=%async_computation.23 | async-start | bytes 19009536 | tf_op jit(solution)/shard_map/all_gather | solution.py:18
  52.5 48.2 %copy-start.43 = (f32[16,1,128]{2,1,0:T(1,128)}, f32[16,1,128]{2,1,0:T(1,128)S(1)}, u32[]{:S(2)}) copy-start(f32[16,1,128]{2,1,0:T(1,128)S(1)} %convert_element_type.122) | copy-start | bytes 24580
  52.5 511.4 %copy-start.53 = (f32[273]{0:T(512)}, f32[273]{0:T(512)S(1)}, u32[]{:S(2)}) copy-start(f32[273]{0:T(512)S(1)} %pad.5.clone) | copy-start | bytes 3280
  54.6 46.1 %copy-start.51 = (f32[512]{0:T(512)}, f32[512]{0:T(512)S(1)}, u32[]{:S(2)}) copy-start(f32[512]{0:T(512)S(1)} %add_rsqrt_fusion.1) | copy-start | bytes 6148
  55.3 58.4 %copy-start.49 = (f32[512]{0:T(512)}, f32[512]{0:T(512)S(1)}, u32[]{:S(2)}) copy-start(f32[512]{0:T(512)S(1)} %get-tuple-element.447) | copy-start | bytes 6148
  55.3 508.7 %copy-start.56 = (f32[512]{0:T(512)}, f32[512]{0:T(512)S(1)}, u32[]{:S(2)}) copy-start(f32[512]{0:T(512)S(1)} %get-tuple-element.446) | copy-start | bytes 6148
  99.9 193.4 %copy-start = (bf16[512,2048]{1,0:T(8,128)(2,1)}, bf16[512,2048]{1,0:T(8,128)(2,1)S(1)}, u32[]{:S(2)}) copy-start(bf16[512,2048]{1,0:T(8,128)(2,1)S(1)} %fusion.13) | copy-start | bytes 6291460
  101.4 12.3 copy-start.21
  111.6 62.7 %copy-start.58 = (u32[32]{0:T(128)S(1)}, u32[32]{0:T(128)}, u32[]{:S(2)}) copy-start(u32[32]{0:T(128)} %constant.131) | copy-start | bytes 388
  111.7 122.6 %copy-start.48 = (bf16[128,128]{1,0:T(8,128)(2,1)S(1)}, bf16[128,128]{1,0:T(8,128)(2,1)}, u32[]{:S(2)}) copy-start(bf16[128,128]{1,0:T(8,128)(2,1)} %param.19) | copy-start | bytes 98308
  112.9 475.7 %all-gather.16.cloned.1.call-start = ((), (), s32[]{:S(2)}) async-start(), calls=%async_computation.8 | async-start | bytes 4456448 | tf_op jit(solution)/shard_map/all_gather | solution.py:118
  113.6 521.1 %all-reduce.10.cloned.1.call-start = ((), (), s32[]{:S(2)}) async-start(), calls=%async_computation.9 | async-start | bytes 8388608 | tf_op jit(solution)/shard_map/psum | solution.py:148
  296.8 267.2 %copy-start.39 = (f32[512,8,16]{0,2,1:T(8,128)}, f32[512,8,16]{0,2,1:T(8,128)S(1)}, u32[]{:S(2)}) copy-start(f32[512,8,16]{0,2,1:T(8,128)S(1)} %broadcast_multiply_fusion) | copy-start | bytes 786436
  296.8 6.1 copy-start.35
  557.9 13.6 copy-start.61
  557.9 6.1 copy-start.19
  564.0 7.6 copy-start.45
  571.5 17.1 copy-start.13
  595.1 39.7 %copy-start.4 = (bf16[512,2048]{1,0:T(8,128)(2,1)S(1)}, bf16[512,2048]{1,0:T(8,128)(2,1)}, u32[]{:S(2)}) copy-start(bf16[512,2048]{1,0:T(8,128)(2,1)} %param.16) | copy-start | bytes 6291460
  595.1 173.2 %all-gather.18.cloned.1.call-start = ((), (), s32[]{:S(2)}) async-start(), calls=%async_computation.10 | async-start | bytes 12255232 | tf_op jit(solution)/shard_map/all_gather | solution.py:151
  595.7 315.9 %all-gather.20.cloned.1.call-start = ((), (), s32[]{:S(2)}) async-start(), calls=%async_computation.11 | async-start | bytes 12255232 | tf_op jit(solution)/shard_map/all_gather | solution.py:152
  596.3 499.2 %all-gather.22.cloned.1.call-start = ((), (), s32[]{:S(2)}) async-start(), calls=%async_computation.12 | async-start | bytes 12255232 | tf_op jit(solution)/shard_map/all_gather | solution.py:153
  597.1 562.5 %all-reduce.14.cloned.1.call-start = ((), (), s32[]{:S(2)}) async-start(), calls=%async_computation.14 | async-start | bytes 8388608 | tf_op jit(solution)/shard_map/psum | solution.py:187
  640.3 128.0 %copy-start.24 = (bf16[512,2048]{1,0:T(8,128)(2,1)}, bf16[512,2048]{1,0:T(8,128)(2,1)S(1)}, u32[]{:S(2)}) copy-start(bf16[512,2048]{1,0:T(8,128)(2,1)S(1)} %multiply_convert_fusion.3) | copy-start | bytes 6291460
  779.4 316.1 %copy-start.23 = (bf16[512,2048]{1,0:T(8,128)(2,1)S(1)}, bf16[512,2048]{1,0:T(8,128)(2,1)}, u32[]{:S(2)}) copy-start(bf16[512,2048]{1,0:T(8,128)(2,1)} %param.27) | copy-start | bytes 6291460
  1111.3 10.9 copy-start.64
  1132.8 52.1 %all-reduce.12.cloned.1.call-start = ((), (), s32[]{:S(2)}) async-start(), calls=%async_computation.13 | async-start | bytes 4194304 | tf_op jit(solution)/shard_map/psum | solution.py:165
  1143.8 431.7 %all-gather.26.cloned.1.call-start = ((), (), s32[]{:S(2)}) async-start(), calls=%async_computation.24 | async-start | bytes 19009536 | tf_op jit(solution)/shard_map/all_gather | solution.py:18
  1185.0 6.1 copy-start.9
  1185.0 6.7 copy-start.25
  1200.8 564.6 %all-reduce.16.cloned.1.call-start = ((), (), s32[]{:S(2)}) async-start(), calls=%async_computation.15 | async-start | bytes 8388608 | tf_op jit(solution)/shard_map/psum | solution.py:232
  1200.9 65.5 %copy-start.28 = (f32[512,1024]{0,1:T(8,128)S(1)}, f32[512,1024]{0,1:T(8,128)}, u32[]{:S(2)}) copy-start(f32[512,1024]{0,1:T(8,128)} %copy-done.27) | copy-start | bytes 6291460
  1274.9 11.0 copy-start.33
  1292.0 283.4 %copy-start.62 = (f32[16]{0:T(128)S(1)}, f32[16]{0:T(128)}, u32[]{:S(2)}) copy-start(f32[16]{0:T(128)} %copy-done.61) | copy-start | bytes 196
  1575.5 62.5 %copy-start.50 = (f32[512]{0:T(512)S(1)}, f32[512]{0:T(512)}, u32[]{:S(2)}) copy-start(f32[512]{0:T(512)} %copy-done.49) | copy-start | bytes 6148
  1641.4 8.4 slice-start
  1642.3 7.4 slice-start.1
  1659.2 198.2 %reduce-scatter.8.cloned.1.call-start = ((), (), s32[]{:S(2)}) async-start(), calls=%async_computation.16 | async-start | bytes 1114112 | tf_op jit(solution)/shard_map/reduce_scatter | solution.py:238
  1662.5 287.9 %reduce-scatter.14.cloned.1.call-start = ((), (), s32[]{:S(2)}) async-start(), calls=%async_computation.19 | async-start | bytes 8912896 | tf_op jit(solution)/shard_map/reduce_scatter | solution.py:241
  1671.1 362.3 %reduce-scatter.10.cloned.1.call-start = ((), (), s32[]{:S(2)}) async-start(), calls=%async_computation.17 | async-start | bytes 1114112 | tf_op jit(solution)/shard_map/reduce_scatter | solution.py:239
  1672.9 832.6 %reduce-scatter.16.cloned.1.call-start = ((), (), s32[]{:S(2)}) async-start(), calls=%async_computation.20 | async-start | bytes 24510464 | tf_op jit(solution)/shard_map/reduce_scatter | solution.py:193
  1687.7 1300.3 %reduce-scatter.18.cloned.1.call-start = ((), (), s32[]{:S(2)}) async-start(), calls=%async_computation.21 | async-start | bytes 24510464 | tf_op jit(solution)/shard_map/reduce_scatter | solution.py:194
  1701.1 1769.5 %reduce-scatter.20.cloned.1.call-start = ((), (), s32[]{:S(2)}) async-start(), calls=%async_computation.22 | async-start | bytes 24510464 | tf_op jit(solution)/shard_map/reduce_scatter | solution.py:195
  1714.4 1943.6 %reduce-scatter.12.cloned.1.call-start = ((), (), s32[]{:S(2)}) async-start(), calls=%async_computation.18 | async-start | bytes 8912896 | tf_op jit(solution)/shard_map/reduce_scatter | solution.py:240
  1721.4 44.1 %copy-start.5 = (bf16[512,2048]{1,0:T(8,128)(2,1)S(1)}, bf16[512,2048]{1,0:T(8,128)(2,1)}, u32[]{:S(2)}) copy-start(bf16[512,2048]{1,0:T(8,128)(2,1)} %param.16) | copy-start | bytes 6291460
  1721.4 44.1 %copy-start.44 = (f32[16,1,128]{2,1,0:T(1,128)S(1)}, f32[16,1,128]{2,1,0:T(1,128)}, u32[]{:S(2)}) copy-start(f32[16,1,128]{2,1,0:T(1,128)} %copy-done.43) | copy-start | bytes 24580
  1721.4 44.1 %copy-start.52 = (f32[512]{0:T(512)S(1)}, f32[512]{0:T(512)}, u32[]{:S(2)}) copy-start(f32[512]{0:T(512)} %copy-done.51) | copy-start | bytes 6148
  (39 other events, 115.1 us)
Sparse Core Ops, SparseCore 0:
  10.8 83.7 all-gather.13
  113.0 382.4 all-gather.23
  498.3 90.3 all-gather.15
  595.3 26.6 all-reduce.9
  624.9 143.3 all-gather.17
  771.3 140.3 all-gather.19
  914.7 180.7 all-gather.21
  1133.0 26.6 all-reduce.13
  1162.5 22.3 all-reduce.11
  1200.9 374.4 all-gather.25
  1659.3 29.6 all-reduce.15
  1691.7 78.9 reduce-scatter.7
  1773.6 176.7 reduce-scatter.13
  1953.2 80.1 reduce-scatter.9
  2036.1 469.3 reduce-scatter.15
  2508.2 479.7 reduce-scatter.17
  2990.7 479.7 reduce-scatter.19
  3473.3 184.5 reduce-scatter.11
where the time goes:
time: 3680 us; the launch traced here: 3670 us
  waiting for transfers between devices  2750 us (75%)
  blocking collectives  476 us (13%)
  matrix products  232 us (6%)
  other arithmetic  91.6 us (2%)
  local copies, waits for them, and re-layouts  78 us (2%)
    reduce_scatter x1, waiting for transfers between devices, shards(): lax.psum_scatter(down_grad, 'seq', scatter_dimension=1, tiled=True)  483 us
    reduce_scatter x1, waiting for transfers between devices, shards(): lax.psum_scatter(up_grad, 'seq', scatter_dimension=0, tiled=True)  483 us
    reduce_scatter x1, waiting for transfers between devices, shards(): lax.psum_scatter(gate_grad, 'seq', scatter_dimension=0, tiled=True)  472 us
    all_gather x2, waiting for transfers between devices, entering(): everything = jax.tree.map(lambda part: lax.all_gather(part, axis), value)  458 us
    reduce_scatter x1, waiting for transfers between devices, shards(): lax.psum_scatter(value_grad, 'seq', scatter_dimension=0, tiled=True)  187 us
    all_gather x1, waiting for transfers between devices, shards(): lax.all_gather(w_down, 'seq', axis=1, tiled=True)  171 us
    unnamed x2, blocking collectives  139 us
    all_gather x1, waiting for transfers between devices, shards(): lax.all_gather(w_up, 'seq', axis=0, tiled=True)  132 us
  transfers between devices with their start and end apart: 18, of which 14 were waited for; matrix products, arithmetic and copies ran while one was open for 7% of the time, Pallas kernels for 0%

commit v1 on v0

v1 whole, which is shorter than its diff:
```python
import functools
import math

import jax
import jax.numpy as jnp
import numpy as np
from jax import lax
from jax.experimental import pallas as pl
from jax.experimental.pallas import tpu as pltpu
from jax.sharding import PartitionSpec as P

H = 16
FD = 16
DV = 128
PLANE = 4
FE = 160
F32, BF = jnp.float32, jnp.bfloat16
NN = (((1,), (0,)), ((), ()))
NT = (((1,), (1,)), ((), ()))
TN = (((0,), (0,)), ((), ()))
LANE_ONE = 64
VMEM = 48 * 2**20


def dot(a, b, dims=NN):
    return lax.dot_general(a, b, dims, preferred_element_type=F32)


def feature_maps():
    qa, qb, ka, kb = (np.zeros((2, 128, FE), np.float32) for _ in range(4))
    q_to_k, k_to_q = (np.zeros((2, 128, 128), np.float32) for _ in range(2))
    for h in range(2):
        q0, k0, f = h * FD, 2 * FD + h * FD, 0
        for i in range(FD):
            for j in range(i, FD):
                qa[h, q0 + i, f] = 1 / 32 if i == j else 1 / 16
                qb[h, q0 + j, f] = 1
                ka[h, k0 + i, f] = kb[h, k0 + j, f] = 1
                f += 1
        for i in range(FD):
            qa[h, q0 + i, f], qb[h, LANE_ONE, f] = 1 / 4, 1
            ka[h, k0 + i, f] = kb[h, LANE_ONE, f] = 1
            f += 1
            q_to_k[h, q0 + i, k0 + i] = k_to_q[h, k0 + i, q0 + i] = 1 / 4
        for m in (qa, qb, ka, kb):
            m[h, LANE_ONE, f] = 1
    wide = [np.pad(m, ((0, 0), (0, 0), (0, 256 - FE))) for m in (qa, qb, ka, kb)]
    one = np.zeros((2, 128, 128), np.float32)
    one[:, LANE_ONE, 0] = 1
    both = np.concatenate([*wide, q_to_k, k_to_q, one], axis=-1)
    return jnp.asarray(both, BF)


def read_maps(maps, h):
    cuts = [(256 * i, FE) for i in range(4)] + [(1024, 128), (1152, 128)]
    return [maps[h, :, a : a + n] for a, n in cuts]


def start_of(sc, n_seq, pos):
    best = jnp.zeros_like(pos)
    for k in range(n_seq):
        at = sc[2 + k]
        best = jnp.where(at <= pos, at, best)
    return best


class Chunk:
    def __init__(self, sc, n_seq, i, rows):
        self.first = sc[1] + i * rows
        self.last = self.first + rows - 1
        pos = self.first + lax.broadcasted_iota(jnp.int32, (rows, 1), 0)
        self.pos = pos
        self.start = start_of(sc, n_seq, pos)
        self.last_start = start_of(sc, n_seq, self.last)
        self.before_start = start_of(sc, n_seq, self.first - 1)
        self.carried = (self.start < self.first).astype(F32)
        self.tail = (self.start == self.last_start).astype(F32)
        self.keep = (self.last_start < self.first).astype(F32)
        self.rows = rows

    def causal(self):
        earlier = self.first + lax.broadcasted_iota(jnp.int32, (self.rows, self.rows), 1)
        return (earlier <= self.pos) & (earlier >= self.start)


def query_key(qkv):
    block = qkv[:, 2 * DV : 3 * DV]
    lane = lax.broadcasted_iota(jnp.int32, block.shape, 1)
    one = jnp.where(lane == LANE_ONE, 1.0, 0.0).astype(BF)
    return jnp.where(lane < LANE_ONE, block, one)


def one_column(qk, maps):
    return dot(qk, maps[0, :, 1280:1408]).astype(BF)


def with_one(value, ones):
    return jnp.concatenate([value, ones], axis=1)


def project_kernel(x_ref, gain_ref, w_ref, normed_ref, qkv_ref):
    x = x_ref[0].astype(F32)
    inv = lax.rsqrt(jnp.mean(x * x, axis=-1, keepdims=True) + 1e-05)
    normed = (x * inv * gain_ref[...]).astype(BF)
    normed_ref[0] = normed
    qkv_ref[0] = dot(normed, w_ref[...]).astype(BF)


def states_kernel(n_seq, sc, qkv_ref, maps, before_ref, total_ref, state):
    i = pl.program_id(0)

    @pl.when(i == 0)
    def _():
        state[...] = jnp.zeros_like(state)

    qkv = qkv_ref[0]
    ch = Chunk(sc, n_seq, i, qkv.shape[0])
    qk = query_key(qkv)
    ones = one_column(qk, maps)
    for h in range(2):
        _, _, ka, kb, _, _ = read_maps(maps, h)
        before_ref[0, h] = state[h].astype(BF)
        feat = (dot(qk, ka) * dot(qk, kb) * ch.tail).astype(BF)
        new = dot(feat, with_one(qkv[:, h * DV : (h + 1) * DV], ones), TN) + ch.keep * state[h]
        state[h] = new
        total_ref[h] = new.astype(BF)


def attend_kernel(n_seq, slot, sc, qkv_ref, before_ref, enter_ref, maps, wo_ref, out1, out0, mixed_ref, den_ref):
    g = pl.program_id(0)
    half = pl.num_programs(0) // 2
    qkv = qkv_ref[0]
    rows = qkv.shape[0]
    ch = Chunk(sc, n_seq, slot(g) ^ sc[0], rows)
    alive = (ch.before_start < sc[1]).astype(F32)
    qk = query_key(qkv)
    ones = one_column(qk, maps)
    causal = ch.causal()
    dens = []
    for h in range(2):
        qa, qb, _, _, q_to_k, _ = read_maps(maps, h)
        s = dot(dot(qk, q_to_k).astype(BF), qk, NT)
        w = jnp.where(causal, 1.0 + s + 0.5 * s * s, 0.0).astype(BF)
        feat = (dot(qk, qa) * dot(qk, qb) * ch.carried).astype(BF)
        state = (before_ref[0, h].astype(F32) + alive * enter_ref[h].astype(F32)).astype(BF)
        num = dot(w, with_one(qkv[:, h * DV : (h + 1) * DV], ones)) + dot(feat, state)
        den = num[:, DV : DV + 1]
        mixed_ref[0, :, h * DV : (h + 1) * DV] = (num[:, :DV] / den).astype(BF)
        dens.append(den)
    lane = lax.broadcasted_iota(jnp.int32, (rows, 128), 1)
    den_ref[0] = jnp.where(lane == 0, dens[0], dens[1])
    part = dot(mixed_ref[0], wo_ref[...], NT).astype(BF)

    @pl.when(g < half)
    def _():
        out1[0] = part

    @pl.when(g >= half)
    def _():
        out0[0] = part


def mlp_kernel(n_ref, cot_ref, wgu_ref, wd_ref, h_ref, ggu_ref, out1, out0):
    g = pl.program_id(0)
    half = pl.num_programs(0) // 2
    main = (wgu_ref.shape[1] - 128) // 2
    gu = dot(n_ref[0], wgu_ref[...])
    gh = dot(cot_ref[0], wd_ref[...], NT)

    def parts(gate, up, grad):
        sig = 1.0 / (1.0 + jnp.exp(-gate))
        silu = gate * sig
        return silu * up, grad * up * sig * (1.0 + gate * (1.0 - sig)), grad * silu

    hid, g_gate, g_up = parts(gu[:, :main], gu[:, main : 2 * main], gh[:, :main])
    h_ref[0, :, :main] = hid.astype(BF)
    ggu_ref[0, :, :main] = g_gate.astype(BF)
    ggu_ref[0, :, main : 2 * main] = g_up.astype(BF)
    rest = gu[:, 2 * main :]
    hid, g_gate, g_up = parts(rest, pltpu.roll(rest, 64, 1), gh[:, main:])
    low = lax.broadcasted_iota(jnp.int32, hid.shape, 1) < 64
    h_ref[0, :, main:] = jnp.where(low, hid, 0.0).astype(BF)
    ggu_ref[0, :, 2 * main :] = jnp.where(low, g_gate, pltpu.roll(g_up, 64, 1)).astype(BF)
    part = dot(ggu_ref[0], wgu_ref[...], NT).astype(BF)

    @pl.when(g < half)
    def _():
        out1[0] = part

    @pl.when(g >= half)
    def _():
        out0[0] = part


def grads_in_kernel(n_seq, sc, ga_ref, wo_ref, qkv_ref, mixed_ref, den_ref, maps, gaug_ref, after_ref, total_ref, state):
    k, n = pl.program_id(0), pl.num_programs(0)
    i = n - 1 - k

    @pl.when(k == 0)
    def _():
        state[...] = jnp.zeros_like(state)

    qkv = qkv_ref[0]
    rows = qkv.shape[0]
    ch = Chunk(sc, n_seq, i, rows)
    qk = query_key(qkv)
    gm = dot(ga_ref[0], wo_ref[...])
    lane = lax.broadcasted_iota(jnp.int32, (rows, 128), 1)
    for h in range(2):
        qa, qb, _, _, _, _ = read_maps(maps, h)
        den = den_ref[0, :, h : h + 1]
        grad = gm[:, h * DV : (h + 1) * DV] / den
        delta = -jnp.sum(grad * mixed_ref[0, :, h * DV : (h + 1) * DV].astype(F32), axis=1, keepdims=True)
        gaug = jnp.concatenate([grad, jnp.where(lane == 0, delta, 0.0)], axis=1).astype(BF)
        gaug_ref[0, :, h * 2 * DV : (h + 1) * 2 * DV] = gaug
        after_ref[0, h] = state[h].astype(BF)
        feat = (dot(qk, qa) * dot(qk, qb) * ch.carried).astype(BF)
        new = dot(feat, gaug, TN) + ch.keep * state[h]
        state[h] = new
        total_ref[h] = new.astype(BF)


def grads_kernel(
    n_seq, slot, sc, qkv_ref, gaug_ref, before_ref, enter_ref, after_ref, leave_ref, maps, w_ref, out1, out0, dqkv_ref
):
    g = pl.program_id(0)
    half = pl.num_programs(0) // 2
    qkv = qkv_ref[0]
    rows = qkv.shape[0]
    ch = Chunk(sc, n_seq, slot(g) ^ sc[0], rows)
    group_last = sc[1] + pl.num_programs(0) * rows - 1
    alive = (ch.before_start < sc[1]).astype(F32)
    alive_after = (start_of(sc, n_seq, group_last) <= ch.last).astype(F32)
    qk = query_key(qkv)
    ones = one_column(qk, maps)
    causal = ch.causal()
    dqk = jnp.zeros((rows, 128), F32)
    for h in range(2):
        qa, qb, ka, kb, q_to_k, k_to_q = read_maps(maps, h)
        value = with_one(qkv[:, h * DV : (h + 1) * DV], ones)
        gaug = gaug_ref[0, :, h * 2 * DV : (h + 1) * 2 * DV]
        quarter = dot(qk, q_to_k).astype(BF)
        s = dot(quarter, qk, NT)
        w = jnp.where(causal, 1.0 + s + 0.5 * s * s, 0.0).astype(BF)
        ds = jnp.where(causal, dot(gaug, value, NT) * (1.0 + s), 0.0).astype(BF)
        dqk += dot(ds, dot(qk, k_to_q).astype(BF)) + dot(ds, quarter, TN)
        before = (before_ref[0, h].astype(F32) + alive * enter_ref[h].astype(F32)).astype(BF)
        after = (after_ref[0, h].astype(F32) + alive_after * leave_ref[h].astype(F32)).astype(BF)
        a, b = dot(qk, qa), dot(qk, qb)
        df = dot(gaug, before, NT) * ch.carried
        dqk += dot((df * b).astype(BF), qa, NT) + dot((df * a).astype(BF), qb, NT)
        a, b = dot(qk, ka), dot(qk, kb)
        df = dot(value, after, NT) * ch.tail
        dqk += dot((df * b).astype(BF), ka, NT) + dot((df * a).astype(BF), kb, NT)
        feat = (a * b * ch.tail).astype(BF)
        dv = dot(w, gaug[:, :DV], TN) + dot(feat, after[:, :DV])
        dqkv_ref[0, :, h * DV : (h + 1) * DV] = dv.astype(BF)
    lane = lax.broadcasted_iota(jnp.int32, dqk.shape, 1)
    dqkv_ref[0, :, 2 * DV :] = jnp.where(lane < LANE_ONE, dqk, 0.0).astype(BF)
    part = dot(dqkv_ref[0], w_ref[...], NT).astype(BF)

    @pl.when(g < half)
    def _():
        out1[0] = part

    @pl.when(g >= half)
    def _():
        out0[0] = part


class Place:
    def __init__(self):
        self.n = lax.axis_size("seq")
        self.groups = self.n // PLANE
        s = lax.axis_index("seq")
        self.s, self.z, self.p, self.c = s, s // PLANE, s % PLANE, lax.axis_index("head")

    def flip(self, v, bits):
        return lax.ppermute(v, "seq", [(s, s ^ bits) for s in range(self.n)])

    def core(self, v):
        return lax.ppermute(v, "head", [(0, 1), (1, 0)])

    def along(self, v, step, sources):
        pairs = [
            (s, s + step * PLANE)
            for s in range(self.n)
            if s // PLANE in sources and 0 <= s // PLANE + step < self.groups
        ]
        return lax.ppermute(v, "seq", pairs)

    def spread(self, pack):
        own = [lax.dynamic_index_in_dim(pack, self.p ^ j, 0, keepdims=False) for j in range(PLANE)]
        got = [own[0]] + [self.flip(own[j], j) for j in range(1, PLANE)]
        return [lax.select_n(self.p, *[got[i ^ q] for q in range(PLANE)]) for i in range(PLANE)]

    def gather_line(self, slab):
        up, down, top = [slab], [slab], self.groups
        for k in range(1, top):
            up.append(self.along(up[-1], 1, range(k - 1, top)))
            down.append(self.along(down[-1], -1, range(0, top - k + 1)))
        return [
            lax.select_n(self.z, *[up[q - i] if q >= i else down[i - q] for q in range(top)]) for i in range(top)
        ]

    def scatter_line(self, piece):
        top = self.groups
        total = piece(self.z).astype(F32)
        for step in (1, -1):
            got = None
            for k in range(1, top):
                far = top - k if step == 1 else k - top
                term = piece(jnp.clip(self.z + far, 0, top - 1))
                if got is not None:
                    term = (term.astype(F32) + got.astype(F32)).astype(BF)
                sources = range(0, k) if step == 1 else range(top - k, top)
                got = self.along(term, step, sources)
            if got is not None:
                total = total + got.astype(F32)
        return total

    def gather8(self, mine, other=None):
        cut = mine.shape[0] // 2
        mx, my = self.flip(mine, 1), self.flip(mine, 2)
        da, db = self.flip(my[:cut], 1), self.flip(mx[cut:], 2)
        other = self.core(mine) if other is None else other
        ox, oy, oda, odb = (self.core(v) for v in (mx, my, da, db))
        whole = jnp.concatenate([mine, other, mx, ox, my, oy, da, db, oda, odb], axis=0)
        return whole.reshape(2 * PLANE, mine.shape[0], mine.shape[1])

    def reduce8(self, other_half, own_half):
        total = own_half.astype(F32) + self.core(other_half).astype(F32)
        cut = total.shape[1] // 2
        a, b = total[:, :cut], total[:, cut:]
        got_x = self.flip(a[1::2].astype(BF), 1).astype(F32)
        got_y = self.flip(b[2:].astype(BF), 2).astype(F32)
        last_y = self.flip((a[2] + got_x[1]).astype(BF), 2).astype(F32)
        last_x = self.flip((b[1] + got_y[1]).astype(BF), 1).astype(F32)
        return jnp.concatenate([a[0] + got_x[0] + last_y, b[0] + got_y[0] + last_x], axis=0)

    def both(self, mine):
        other = self.core(mine)
        return jnp.concatenate(
            [lax.select_n(self.c, mine, other), lax.select_n(self.c, other, mine)], axis=0
        )


def cost(flops, nbytes):
    return pl.CostEstimate(flops=int(flops), bytes_accessed=int(nbytes), transcendentals=0)


def rms_parts(rows):
    return lax.rsqrt(jnp.mean(rows * rows, axis=-1, keepdims=True) + 1e-05)


def rms_back(grad_normed, x_hat, inv_rms, gain_vec):
    grad_hat = grad_normed * gain_vec
    return inv_rms * (grad_hat - x_hat * jnp.mean(grad_hat * x_hat, axis=-1, keepdims=True))


def split_hidden(w):
    rows, cols = w.shape
    main = cols // PLANE // 128 * 128
    rest = (cols - PLANE * main) // PLANE
    first = w[:, : PLANE * main].reshape(rows, PLANE, main)
    return first.transpose(1, 0, 2), w[:, PLANE * main :].reshape(rows, PLANE, rest).transpose(1, 0, 2)


def shards(
    layer_input,
    seq_lengths,
    gain_attn,
    w_query,
    w_key,
    w_value,
    w_out,
    gain_mlp,
    w_gate,
    w_up,
    w_down,
    cotangent,
):
    me = Place()
    rows, width = layer_input.shape
    half_rows = rows // 2
    slots = 2 * PLANE
    group_rows = PLANE * rows
    n_seq = seq_lengths.shape[0]
    db = w_query.shape[0]
    hidden = w_down.shape[0]
    main = hidden // PLANE // 128 * 128
    rest = hidden // PLANE - main
    assert H == slots * 2 and rest == 64
    own8 = me.p * 2 + me.c

    k = jnp.arange(n_seq)
    starts = jnp.sum(jnp.where(k[None, :] < k[:, None], seq_lengths[None, :], 0), axis=1)
    first = me.z * group_rows
    sc = jnp.concatenate([jnp.stack([own8, first]).astype(jnp.int32), starts.astype(jnp.int32)])
    maps = feature_maps()

    def slot_first_other(g):
        return (g % PLANE) * 2 + 1 - g // PLANE

    def by_part(w, parts=PLANE):
        return w.reshape(w.shape[0], parts, w.shape[1] // parts).transpose(1, 0, 2)

    gains = jnp.stack([gain_attn, gain_mlp], axis=1)
    fill = jnp.concatenate([gains, jnp.zeros((db, 62), BF)], axis=1)
    attn_pack = jnp.concatenate(
        [by_part(w_value), by_part(w_query), by_part(w_key), jnp.broadcast_to(fill, (PLANE, db, 64)), by_part(w_out.T)],
        axis=2,
    )
    g_main, g_rest = split_hidden(w_gate)
    u_main, u_rest = split_hidden(w_up)
    gu_pack = jnp.concatenate([g_main, u_main, g_rest, u_rest], axis=2)
    down_pack = jnp.concatenate(
        [w_down[: PLANE * main].reshape(PLANE, main, db), w_down[PLANE * main :].reshape(PLANE, rest, db)], axis=1
    )
    attn_w = jnp.concatenate(me.gather_line(jnp.concatenate(me.spread(attn_pack), axis=0)), axis=0)
    gu_w = jnp.concatenate(me.gather_line(jnp.concatenate(me.spread(gu_pack), axis=0)), axis=0)
    down_w = jnp.concatenate(me.gather_line(jnp.concatenate(me.spread(down_pack), axis=1)), axis=1)
    down_w = jnp.concatenate([down_w, jnp.zeros((64, width), BF)], axis=0)
    w_qkv, w_o = attn_w[:, : 3 * DV], attn_w[:, 3 * DV :]
    gain_one = attn_w[:, 2 * DV + 64].astype(F32)[None, :]
    gain_two = attn_w[:, 2 * DV + 65].astype(F32)[None, :]

    def my_half(v):
        return lax.dynamic_slice_in_dim(v, me.c * half_rows, half_rows, 0)

    def other_half(v):
        return lax.dynamic_slice_in_dim(v, (1 - me.c) * half_rows, half_rows, 0)

    x_all = me.gather8(my_half(layer_input), other_half(layer_input))
    cot_all = me.gather8(my_half(cotangent), other_half(cotangent))

    params = pltpu.CompilerParams(dimension_semantics=("arbitrary",), vmem_limit_bytes=VMEM)
    row_block = lambda cols: pl.BlockSpec((1, half_rows, cols), lambda g: (g, 0, 0))
    whole = lambda *shape: pl.BlockSpec(shape, lambda *_: (0,) * len(shape))

    normed, qkv = pl.pallas_call(
        project_kernel,
        grid=(slots,),
        in_specs=[row_block(width), whole(1, width), whole(width, 3 * DV)],
        out_specs=[row_block(width), row_block(3 * DV)],
        out_shape=[
            jax.ShapeDtypeStruct((slots, half_rows, width), BF),
            jax.ShapeDtypeStruct((slots, half_rows, 3 * DV), BF),
        ],
        compiler_params=params,
        cost_estimate=cost(2 * group_rows * width * 3 * DV, 4 * group_rows * width),
        name="project",
    )(x_all, gain_one, w_qkv)

    map_spec = whole(*maps.shape)
    state_spec = whole(2, FE, 2 * DV)
    state_shape = jax.ShapeDtypeStruct((2, FE, 2 * DV), BF)
    states_shape = jax.ShapeDtypeStruct((slots, 2, FE, 2 * DV), BF)

    def in_order(cols):
        return pl.BlockSpec((1, half_rows, cols), lambda i, s: (i ^ s[0], 0, 0))

    before, total = pl.pallas_call(
        functools.partial(states_kernel, n_seq),
        grid_spec=pltpu.PrefetchScalarGridSpec(
            num_scalar_prefetch=1,
            grid=(slots,),
            in_specs=[in_order(3 * DV), map_spec],
            out_specs=[pl.BlockSpec((1, 2, FE, 2 * DV), lambda i, s: (i, 0, 0, 0)), state_spec],
            scratch_shapes=[pltpu.VMEM((2, FE, 2 * DV), F32)],
        ),
        out_shape=[states_shape, state_shape],
        compiler_params=params,
        cost_estimate=cost(slots * 2e8, 2**21),
        name="states",
    )(sc, qkv, maps)

    def start_at(pos):
        return jnp.max(jnp.where(starts <= pos, starts, 0))

    top = me.groups
    reach = start_at(first - 1)
    enter = jnp.zeros((2, FE, 2 * DV), F32)
    for hop in range(1, top):
        got = me.along(total, hop, range(top)).astype(F32)
        live = (me.z >= hop) & (reach < first - (hop - 1) * group_rows)
        enter = enter + jnp.where(live, got, 0.0)
    enter = enter.astype(BF)

    def any_order(cols):
        return pl.BlockSpec((1, half_rows, cols), lambda g, s: (slot_first_other(g), 0, 0))

    def any_state(g, s):
        return (slot_first_other(g) ^ s[0], 0, 0, 0)

    part_specs = [
        pl.BlockSpec((1, half_rows, width), lambda g, *_: (jnp.minimum(g, PLANE - 1), 0, 0)),
        pl.BlockSpec((1, half_rows, width), lambda g, *_: (jnp.maximum(g - PLANE, 0), 0, 0)),
    ]
    part_shapes = [jax.ShapeDtypeStruct((PLANE, half_rows, width), BF)] * 2
    attn_other, attn_own, mixed, den = pl.pallas_call(
        functools.partial(attend_kernel, n_seq, slot_first_other),
        grid_spec=pltpu.PrefetchScalarGridSpec(
            num_scalar_prefetch=1,
            grid=(slots,),
            in_specs=[
                any_order(3 * DV),
                pl.BlockSpec((1, 2, FE, 2 * DV), any_state),
                state_spec,
                map_spec,
                whole(width, 2 * DV),
            ],
            out_specs=[*part_specs, any_order(2 * DV), any_order(128)],
        ),
        out_shape=[
            *part_shapes,
            jax.ShapeDtypeStruct((slots, half_rows, 2 * DV), BF),
            jax.ShapeDtypeStruct((slots, half_rows, 128), F32),
        ],
        compiler_params=params,
        cost_estimate=cost(slots * 8e8, 2**24),
        name="attend",
    )(sc, qkv, before, enter, maps, w_o)

    x_mine = my_half(layer_input).astype(F32)
    resid = x_mine + me.reduce8(attn_other, attn_own)
    inv_two = rms_parts(resid)
    x_hat_two = resid * inv_two
    normed_mlp = me.gather8((x_hat_two * gain_two).astype(BF))

    wide = 2 * main + 2 * rest
    tall = main + 128
    hid, grad_gu, gn_other, gn_own = pl.pallas_call(
        mlp_kernel,
        grid=(slots,),
        in_specs=[
            pl.BlockSpec((1, half_rows, width), lambda g: (slot_first_other(g), 0, 0)),
            pl.BlockSpec((1, half_rows, width), lambda g: (slot_first_other(g), 0, 0)),
            whole(width, wide),
            whole(tall, width),
        ],
        out_specs=[
            pl.BlockSpec((1, half_rows, tall), lambda g: (slot_first_other(g), 0, 0)),
            pl.BlockSpec((1, half_rows, wide), lambda g: (slot_first_other(g), 0, 0)),
            *part_specs,
        ],
        out_shape=[
            jax.ShapeDtypeStruct((slots, half_rows, tall), BF),
            jax.ShapeDtypeStruct((slots, half_rows, wide), BF),
            *part_shapes,
        ],
        compiler_params=params,
        cost_estimate=cost(2 * group_rows * width * (2 * wide + tall), 2**25),
        name="mlp",
    )(normed_mlp, cot_all, gu_w, down_w)

    grad_normed_mlp = me.reduce8(gn_other, gn_own)
    grad_resid = my_half(cotangent).astype(F32) + rms_back(grad_normed_mlp, x_hat_two, inv_two, gain_two)
    grad_attn = me.gather8(grad_resid.astype(BF))

    def flat(v):
        return v.reshape(slots * half_rows, v.shape[2])

    gu_grad = dot(flat(normed_mlp), flat(grad_gu), TN).astype(BF)
    down_grad = dot(flat(hid), flat(cot_all), TN).astype(BF)
    lo = dot(flat(hid), down_w).astype(BF).reshape(PLANE, 2, half_rows, width)
    mlp_sum = me.reduce8(lo[:, 1], lo[:, 0])
    layer_out = me.both((resid + mlp_sum).astype(BF))

    def reverse(cols):
        return pl.BlockSpec((1, half_rows, cols), lambda k, s: ((slots - 1 - k) ^ s[0], 0, 0))

    gaug, after, back_total = pl.pallas_call(
        functools.partial(grads_in_kernel, n_seq),
        grid_spec=pltpu.PrefetchScalarGridSpec(
            num_scalar_prefetch=1,
            grid=(slots,),
            in_specs=[reverse(width), whole(width, 2 * DV), reverse(3 * DV), reverse(2 * DV), reverse(128), map_spec],
            out_specs=[
                reverse(4 * DV),
                pl.BlockSpec((1, 2, FE, 2 * DV), lambda k, s: (slots - 1 - k, 0, 0, 0)),
                state_spec,
            ],
            scratch_shapes=[pltpu.VMEM((2, FE, 2 * DV), F32)],
        ),
        out_shape=[jax.ShapeDtypeStruct((slots, half_rows, 4 * DV), BF), states_shape, state_shape],
        compiler_params=params,
        cost_estimate=cost(slots * 8e8, 2**24),
        name="grads_in",
    )(sc, grad_attn, w_o, qkv, mixed, den, maps)

    leave = jnp.zeros((2, FE, 2 * DV), F32)
    for hop in range(1, top):
        got = me.along(back_total, -hop, range(top)).astype(F32)
        other_first = first + hop * group_rows
        live = (me.z + hop < top) & (start_at(other_first - 1) < first + group_rows)
        leave = leave + jnp.where(live, got, 0.0)
    leave = leave.astype(BF)

    ga_other, ga_own, dqkv = pl.pallas_call(
        functools.partial(grads_kernel, n_seq, slot_first_other),
        grid_spec=pltpu.PrefetchScalarGridSpec(
            num_scalar_prefetch=1,
            grid=(slots,),
            in_specs=[
                any_order(3 * DV),
                any_order(4 * DV),
                pl.BlockSpec((1, 2, FE, 2 * DV), any_state),
                state_spec,
                pl.BlockSpec((1, 2, FE, 2 * DV), any_state),
                state_spec,
                map_spec,
                whole(width, 3 * DV),
            ],
            out_specs=[*part_specs, any_order(3 * DV)],
        ),
        out_shape=[*part_shapes, jax.ShapeDtypeStruct((slots, half_rows, 3 * DV), BF)],
        compiler_params=params,
        cost_estimate=cost(slots * 16e8, 2**24),
        name="grads",
    )(sc, qkv, gaug, before, enter, after, leave, maps, w_qkv)

    grad_normed = me.reduce8(ga_other, ga_own).astype(BF)
    grad_normed_both = me.both(grad_normed).astype(F32)
    grad_resid_both = me.both(grad_resid)
    x_float = layer_input.astype(F32)
    inv_one = rms_parts(x_float)
    input_grad = grad_resid_both + rms_back(grad_normed_both, x_float * inv_one, inv_one, gain_one)

    qkv_grad = dot(flat(normed), flat(dqkv), TN).astype(BF)
    o_grad = dot(flat(grad_attn), flat(mixed), TN).astype(BF)
    attn_grad = jnp.concatenate([qkv_grad, o_grad], axis=1)
    slab = PLANE * db

    def row_piece(v):
        return lambda i: lax.dynamic_slice_in_dim(v, i * slab, slab, 0)

    def col_piece(v):
        return lambda i: lax.dynamic_slice_in_dim(v, i * slab, slab, 1)

    gu_sum = me.scatter_line(row_piece(gu_grad)).astype(BF)
    down_sum = me.scatter_line(col_piece(down_grad[: main + rest])).astype(BF)
    attn_sum = me.scatter_line(row_piece(attn_grad)).astype(BF)
    gu_parts = me.spread(gu_sum.reshape(PLANE, db, wide))
    down_parts = me.spread(down_sum.reshape(main + rest, PLANE, db).transpose(1, 0, 2))
    attn_parts = me.spread(attn_sum.reshape(PLANE, db, 5 * DV))

    def cols(parts, a, b):
        return [v[:, a:b].astype(F32) for v in parts]

    gate_grad = jnp.concatenate(cols(gu_parts, 0, main) + cols(gu_parts, 2 * main, 2 * main + rest), axis=1)
    up_grad = jnp.concatenate(cols(gu_parts, main, 2 * main) + cols(gu_parts, 2 * main + rest, wide), axis=1)
    down_out = jnp.concatenate(
        [v[:main].astype(F32) for v in down_parts] + [v[main:].astype(F32) for v in down_parts], axis=0
    )
    value_grad = jnp.concatenate(cols(attn_parts, 0, 2 * DV), axis=1)
    query_grad = jnp.concatenate(cols(attn_parts, 2 * DV, 2 * DV + 2 * FD), axis=1)
    key_grad = jnp.concatenate(cols(attn_parts, 2 * DV + 2 * FD, 2 * DV + 4 * FD), axis=1)
    out_grad = jnp.concatenate(cols(attn_parts, 3 * DV, 5 * DV), axis=1).T

    def along_cols(*pairs):
        return sum(jnp.sum(w.astype(F32) * grad, axis=1) for w, grad in pairs)

    gain_parts = jnp.stack(
        [
            along_cols((w_query, query_grad), (w_key, key_grad), (w_value, value_grad)),
            along_cols((w_gate, gate_grad), (w_up, up_grad)),
        ]
    )
    gain_sums = gain_parts + me.core(gain_parts)
    gain_one_grad = gain_sums[0] / gain_attn.astype(F32)
    gain_two_grad = gain_sums[1] / gain_mlp.astype(F32)

    den2 = den[:, :, :2]
    ends = jnp.stack([-jnp.min(den2), jnp.max(den2)])
    ends = jnp.broadcast_to(ends[:, None], (2, 128))
    ends = jnp.maximum(ends, me.core(ends))
    ends = jnp.maximum(ends, me.flip(ends, 1))
    ends = jnp.maximum(ends, me.flip(ends, 2))
    best = ends
    for hop in range(1, top):
        for step in (hop, -hop):
            got = me.along(ends, step, range(top))
            ok = (me.z - step >= 0) & (me.z - step < top)
            best = jnp.where(ok, jnp.maximum(best, got), best)
    den_stats = jnp.stack([jnp.log(-best[0, 0]), jnp.log(best[1, 0])])

    return (
        layer_out,
        input_grad,
        gain_one_grad,
        query_grad,
        key_grad,
        value_grad,
        out_grad,
        gain_two_grad,
        gate_grad,
        up_grad,
        down_out,
        den_stats,
    )


def solution(mesh):
    return jax.shard_map(
        shards,
        mesh=mesh,
        in_specs=(
            P("seq", None),
            P(),
            P("seq"),
            P("seq", "head"),
            P("seq", "head"),
            P("seq", "head"),
            P("head", "seq"),
            P("seq"),
            P("seq", "head"),
            P("seq", "head"),
            P("head", "seq"),
            P("seq", None),
        ),
        out_specs=(
            P("seq", None),
            P("seq", None),
            P("seq"),
            P("seq", "head"),
            P("seq", "head"),
            P("seq", "head"),
            P("head", "seq"),
            P("seq"),
            P("seq", "head"),
            P("seq", "head"),
            P("head", "seq"),
            P(),
        ),
        check_vma=False,
    )
```

time: 3680 us -> 996 us (0.27)
  waiting for transfers between devices: 2750 us -> 344 us
  blocking collectives: 476 us -> 0 us
  starting transfers between devices: 0.73 us -> 208 us
  matrix products: 232 us -> 46 us
  Pallas kernels: 0 us -> 118 us
  other arithmetic: 91.6 us -> 153 us
    reduce_scatter x7 -> x0, waiting for transfers between devices: 1800 us -> none  [the longest x1 483 us: shards(): lax.psum_scatter(down_grad, 'seq', scatter_dimension=1, tiled=True)]
    all_gather x7 -> x0, waiting for transfers between devices: 907 us -> none  [the longest x2 458 us: entering(): everything = jax.tree.map(lambda part: lax.all_gather(part, axis), value)]
    ppermute x0 -> x127, waiting for transfers between devices: none -> 344 us  [the longest x48 173 us: along(): return lax.ppermute(v, 'seq', pairs)]
    all_gather x6 -> x0, blocking collectives: 296 us -> none  [the longest x2 115 us: entering(): everything = jax.tree.map(lambda part: lax.all_gather(part, axis), value)]
    ppermute x0 -> x127, starting transfers between devices: none -> 208 us  [the longest x48 148 us: along(): return lax.ppermute(v, 'seq', pairs)]
    dot_general x35 -> x5, matrix products: 232 us -> 46 us  [dot(): return lax.dot_general(a, b, dims, preferred_element_type=F32)]
    unnamed x2 -> x0, blocking collectives: 139 us -> none
    pallas_call x0 -> x6, Pallas kernels: none -> 118 us  [the longest x1 47.4 us: shards(): pl.pallas_call(mlp_kernel, grid=(slots,), in_specs=[pl.BlockSpec((1, half...]
  transfers between devices with their start and end apart: 18 -> 127, of which waited for: 14 -> 45; matrix products, arithmetic and copies ran while one was open for 7% -> 28% of each run, Pallas kernels for 0% -> 12%
where the time goes in v1:
time: 996 us; the launch traced here: 985 us
  waiting for transfers between devices  344 us (35%)
  starting transfers between devices  208 us (21%)
  other arithmetic  153 us (15%)
  Pallas kernels  118 us (12%)
  local copies, waits for them, and re-layouts  107 us (11%)
  matrix products  46 us (5%)
    ppermute x48, waiting for transfers between devices, along(): return lax.ppermute(v, 'seq', pairs)  173 us
    ppermute x52, waiting for transfers between devices, flip(): return lax.ppermute(v, 'seq', [(s, s ^ bits) for s in range(self.n)])  169 us
    ppermute x48, starting transfers between devices, along(): return lax.ppermute(v, 'seq', pairs)  148 us
    ppermute x52, starting transfers between devices, flip(): return lax.ppermute(v, 'seq', [(s, s ^ bits) for s in range(self.n)])  56.5 us
    unnamed x215, local copies, waits for them, and re-layouts  51.3 us
    pallas_call x1, Pallas kernels, shards(): pl.pallas_call(mlp_kernel, grid=(slots,), in_specs=[pl.BlockSpec((1, half...  47.4 us
    dot_general x5, matrix products, dot(): return lax.dot_general(a, b, dims, preferred_element_type=F32)  46 us
    add x4, other arithmetic, reduce8(): total = own_half.astype(F32) + self.core(other_half).astype(F32)  32.1 us
  transfers between devices with their start and end apart: 127, of which 45 were waited for; matrix products, arithmetic and copies ran while one was open for 28% of the time, Pallas kernels for 12%

profile of v1, /device:TPU:0, one launch (start us, length us, event | category | flops | bytes accessed | tf_op | source)
XLA Modules:
  0.0 984.9 jit_solution(14066261666998270758)
XLA Ops:
  13.0 17.3 %collective-permute-done = bf16[256,2048]{1,0:T(8,128)(2,1)} collective-permute-done((bf16[256,2048]{1,0:T(8,128)(2,1)S(1)}, bf16[256,2048]{1,0:T(8,128)(2,1)}, u32[]{:S(2)}, u32[]{:S(2)}) %collective-permute-start) | collective-permute-done | bytes 1048608 | tf_op jit(solution)/shard_map/ppermute | solution.py:279
  30.3 7.5 collective-permute-done.9
  82.7 9.4 collective-permute-done.16
  96.1 6.1 pad_maximum_fusion.1
  102.4 11.2 %project.1 = (bf16[8,256,2048]{2,1,0:T(8,128)(2,1)}, bf16[8,256,384]{2,1,0:T(8,128)(2,1)S(1)}) custom-call(bf16[8,256,2048]{2,1,0:T(8,128)(2,1)} %bitcast.267, f32[1,2048]{1,0:T(1,128)S(1)} %bitcast.237, bf16[2048,384]{1,0:T(8,128)(2,1)S(1)} %slice.478.w_ref), custom_call_target="tpu_custom_call" | custom-call | flops 3221225472 | bytes 16777216 | tf_op jit(solution)/shard_map/project/pallas_call | solution.py:441
  113.5 6.2 states.1
  119.8 19.4 %collective-permute-start.19 = (bf16[2,160,256]{2,1,0:T(8,128)(2,1)S(1)}, bf16[2,160,256]{2,1,0:T(8,128)(2,1)S(1)}, u32[]{:S(2)}, u32[]{:S(2)}) collective-permute-start(bf16[2,160,256]{2,1,0:T(8,128)(2,1)S(1)} %get-tuple-element.32), channel_id=1, source_target_pairs={{0,24},{2,26},{4,28},{6,30},{1,25},{3,27},{5,29},{7,31}} | collective-permute-start | bytes 491528 | tf_op jit(solution)/shard_map/ppermute | solution.py:290
  147.3 14.9 %attend.1 = (bf16[4,256,2048]{2,1,0:T(8,128)(2,1)}, bf16[4,256,2048]{2,1,0:T(8,128)(2,1)}, bf16[8,256,256]{2,1,0:T(8,128)(2,1)S(1)}, f32[8,256,128]{2,1,0:T(8,128)S(1)}) custom-call(s32[6]{0:T(128)S(1)} %pad_add_fusion.sc, bf16[8,256,384]{2,1,0:T(8,128)(2,1)} %copy-done.9, bf16[8,2,160,256]{3,2,1,0:T(8,128)(2,1)S(1)} %get-tuple-element.31.before_ref, ...), custom_call_target="tpu_custom_call" | custom-call | flops 6400000000 | bytes 16777216 | tf_op jit(solution)/shard_map/attend/pallas_call | solution.py:501
  176.3 12.4 %collective-permute-done.43 = bf16[128,1408]{1,0:T(8,128)(2,1)S(1)} collective-permute-done((bf16[128,1408]{1,0:T(8,128)(2,1)}, bf16[128,1408]{1,0:T(8,128)(2,1)S(1)}, u32[]{:S(2)}, u32[]{:S(2)}) %collective-permute-start.43) | collective-permute-done | bytes 360480 | tf_op jit(solution)/shard_map/ppermute | solution.py:279
  192.8 5.8 collective-permute-done.42
  198.6 7.8 collective-permute-start.54
  243.7 9.6 collective-permute-start.45
  253.3 23.4 %collective-permute-done.58 = bf16[704,512]{1,0:T(8,128)(2,1)S(1)} collective-permute-done((bf16[704,512]{1,0:T(8,128)(2,1)}, bf16[704,512]{1,0:T(8,128)(2,1)S(1)}, u32[]{:S(2)}, u32[]{:S(2)}) %collective-permute-start.58) | collective-permute-done | bytes 720928 | tf_op jit(solution)/shard_map/ppermute | solution.py:290
  279.1 7.9 convert_add_fusion.3
  304.8 11.2 %collective-permute-done.21 = bf16[2,128,2048]{2,1,0:T(8,128)(2,1)S(1)} collective-permute-done((bf16[2,128,2048]{2,1,0:T(8,128)(2,1)S(1)}, bf16[2,128,2048]{2,1,0:T(8,128)(2,1)S(1)}, u32[]{:S(2)}, u32[]{:S(2)}) %collective-permute-start.21) | collective-permute-done | bytes 1048608 | tf_op jit(solution)/shard_map/ppermute | solution.py:279
  323.5 10.8 %collective-permute-done.49 = bf16[512,1408]{1,0:T(8,128)(2,1)S(1)} collective-permute-done((bf16[512,1408]{1,0:T(8,128)(2,1)}, bf16[512,1408]{1,0:T(8,128)(2,1)S(1)}, u32[]{:S(2)}, u32[]{:S(2)}) %collective-permute-start.49) | collective-permute-done | bytes 1441824 | tf_op jit(solution)/shard_map/ppermute | solution.py:290
  339.7 28.4 %collective-permute-done.50 = bf16[512,1408]{1,0:T(8,128)(2,1)S(1)} collective-permute-done((bf16[512,1408]{1,0:T(8,128)(2,1)S(1)}, bf16[512,1408]{1,0:T(8,128)(2,1)S(1)}, u32[]{:S(2)}, u32[]{:S(2)}) %collective-permute-start.50) | collective-permute-done | bytes 1441824 | tf_op jit(solution)/shard_map/ppermute | solution.py:290
  379.4 13.5 %pad_maximum_fusion.wgu_ref = bf16[2048,1408]{1,0:T(8,128)(2,1)} fusion(bf16[512,1408]{1,0:T(8,128)(2,1)S(1)} %get-tuple-element.146, bf16[512,1408]{1,0:T(8,128)(2,1)S(1)} %get-tuple-element.145, bf16[512,1408]{1,0:T(8,128)(2,1)S(1)} %get-tuple-element.144, bf16[512,1408]{1,0:T(8,128)(2,1)S(1)} %get-tuple-element.143), kind=kLoop, calls=%fused_computation.12 | loop fusion | flops 23068672 | bytes 11534336 | tf_op jit(solution)/shard_map/concatenate | solution.py:421
  392.9 7.4 collective-permute-start.125
  408.0 47.4 %mlp.1 = (bf16[8,256,768]{2,1,0:T(8,128)(2,1)S(1)}, bf16[8,256,1408]{2,1,0:T(8,128)(2,1)}, bf16[4,256,2048]{2,1,0:T(8,128)(2,1)}, bf16[4,256,2048]{2,1,0:T(8,128)(2,1)}) custom-call(bf16[8,256,2048]{2,1,0:T(8,128)(2,1)} %bitcast.268, bf16[8,256,2048]{2,1,0:T(8,128)(2,1)} %bitcast.22.cot_ref, bf16[2048,1408]{1,0:T(8,128)(2,1)} %pad_maximum_fusion.wgu_ref, ...), custom_call_target="tpu_custom_call" | custom-call | flops 30064771072 | bytes 33554432 | tf_op jit(solution)/shard_map/mlp/pallas_call | solution.py:533
  455.4 9.1 fusion.108
  469.2 15.3 %convolution_convert_fusion.1 = bf16[2048,1408]{1,0:T(8,128)(2,1)S(1)} fusion(bf16[2048,2048]{1,0:T(8,128)(2,1)S(1)} %copy-done.75, bf16[2048,1408]{1,0:T(8,128)(2,1)} %bitcast.271), kind=kOutput, calls=%fused_computation.5 | convolution fusion | flops 11814043648 | bytes 19922944 | tf_op jit(solution)/shard_map/dot_general | solution.py:26
  493.9 8.7 convolution_convert_fusion
  502.6 8.0 collective-permute-start.123
  510.7 26.0 %collective-permute-done.110 = bf16[704,512]{1,0:T(8,128)(2,1)} collective-permute-done((bf16[704,512]{1,0:T(8,128)(2,1)}, bf16[704,512]{1,0:T(8,128)(2,1)}, u32[]{:S(2)}, u32[]{:S(2)}) %collective-permute-start.110) | collective-permute-done | bytes 720928 | tf_op jit(solution)/shard_map/ppermute | solution.py:290
  555.0 9.5 collective-permute-start.100
  574.0 36.7 %collective-permute-done.111 = bf16[704,512]{1,0:T(8,128)(2,1)} collective-permute-done((bf16[704,512]{1,0:T(8,128)(2,1)}, bf16[704,512]{1,0:T(8,128)(2,1)}, u32[]{:S(2)}, u32[]{:S(2)}) %collective-permute-start.111) | collective-permute-done | bytes 720928 | tf_op jit(solution)/shard_map/ppermute | solution.py:290
  628.5 5.5 collective-permute-start.101
  636.9 7.9 convert_add_fusion
  650.9 10.7 %convert_add_fusion.2 = (f32[4,256,2048]{2,1,0:T(8,128)}, bf16[4,256,2048]{2,1,0:T(8,128)(2,1)}) fusion(bf16[4,256,2048]{2,1,0:T(8,128)(2,1)} %collective-permute-done.66, bf16[4,256,2048]{2,1,0:T(8,128)(2,1)} %get-tuple-element.36), kind=kLoop, calls=%fused_computation.2 | loop fusion | flops 8388608 | bytes 20971520 | tf_op jit(solution)/shard_map/add | solution.py:332
  670.0 6.3 collective-permute-done.61
  681.8 15.2 %collective-permute-done.67 = bf16[2,128,2048]{2,1,0:T(8,128)(2,1)S(1)} collective-permute-done((bf16[2,128,2048]{2,1,0:T(8,128)(2,1)S(1)}, bf16[2,128,2048]{2,1,0:T(8,128)(2,1)S(1)}, u32[]{:S(2)}, u32[]{:S(2)}) %collective-permute-start.67) | collective-permute-done | bytes 1048608 | tf_op jit(solution)/shard_map/ppermute | solution.py:279
  700.4 10.1 %collective-permute-done.62 = bf16[128,2048]{1,0:T(8,128)(2,1)S(1)} collective-permute-done((bf16[128,2048]{1,0:T(8,128)(2,1)S(1)}, bf16[128,2048]{1,0:T(8,128)(2,1)S(1)}, u32[]{:S(2)}, u32[]{:S(2)}) %collective-permute-start.62) | collective-permute-done | bytes 524320 | tf_op jit(solution)/shard_map/ppermute | solution.py:279
  712.5 7.3 collective-permute-done.68
  745.9 17.2 %collective-permute-done.73 = bf16[256,2048]{1,0:T(8,128)(2,1)S(1)} collective-permute-done((bf16[256,2048]{1,0:T(8,128)(2,1)S(1)}, bf16[256,2048]{1,0:T(8,128)(2,1)S(1)}, u32[]{:S(2)}, u32[]{:S(2)}) %collective-permute-start.73) | collective-permute-done | bytes 1048608 | tf_op jit(solution)/shard_map/ppermute | solution.py:279
  771.2 7.8 collective-permute-done.77
  787.5 11.9 %grads_in.1 = (bf16[8,256,512]{2,1,0:T(8,128)(2,1)}, bf16[8,2,160,256]{3,2,1,0:T(8,128)(2,1)S(1)}, bf16[2,160,256]{2,1,0:T(8,128)(2,1)S(1)}) custom-call(s32[6]{0:T(128)S(1)} %pad_add_fusion.sc, bf16[8,256,2048]{2,1,0:T(8,128)(2,1)} %bitcast.264, bf16[2048,256]{1,0:T(8,128)(2,1)S(1)} %copy-done.2, bf16[8,256,384]{2,1,0:T(8,128)(2,1)} %copy-done.9, ...), custom_call_target="tpu_custom_call" | custom-call | flops 6400000000 | bytes 16777216 | tf_op jit(solution)/shard_map/grads_in/pallas_call | solution.py:573
  803.6 5.9 convolution_convert_fusion.2
  810.3 6.0 collective-permute-done.82
  816.5 25.9 %grads.1 = (bf16[4,256,2048]{2,1,0:T(8,128)(2,1)}, bf16[4,256,2048]{2,1,0:T(8,128)(2,1)}, bf16[8,256,384]{2,1,0:T(8,128)(2,1)S(1)}) custom-call(s32[6]{0:T(128)S(1)} %pad_add_fusion.sc, bf16[8,256,384]{2,1,0:T(8,128)(2,1)} %copy-done.9, bf16[8,256,512]{2,1,0:T(8,128)(2,1)} %get-tuple-element.40.gaug_ref, bf16[8,2,160,256]{3,2,1,0:T(8,128)(2,1)S(1)} %copy-done.11, ...), custom_call_target="tpu_custom_call" | custom-call | flops 12800000000 | bytes 16777216 | tf_op jit(solution)/shard_map/grads/pallas_call | solution.py:600
  842.4 6.9 bitcast_convert_fusion
  850.6 6.8 collective-permute-start.90
  863.1 7.9 collective-permute-done.90
  885.7 6.2 collective-permute-done.91
  893.7 7.2 collective-permute-start.92
  905.7 7.3 collective-permute-done.92
  928.7 5.6 convert_add_fusion.1
  937.1 18.7 %collective-permute-done.85 = bf16[2,128,2048]{2,1,0:T(8,128)(2,1)S(1)} collective-permute-done((bf16[2,128,2048]{2,1,0:T(8,128)(2,1)S(1)}, bf16[2,128,2048]{2,1,0:T(8,128)(2,1)S(1)}, u32[]{:S(2)}, u32[]{:S(2)}) %collective-permute-start.85) | collective-permute-done | bytes 1048608 | tf_op jit(solution)/shard_map/ppermute | solution.py:279
  (610 shorter events, 380.3 us)
Async XLA Ops:
  3.3 27.0 %collective-permute-start = (bf16[256,2048]{1,0:T(8,128)(2,1)S(1)}, bf16[256,2048]{1,0:T(8,128)(2,1)}, u32[]{:S(2)}, u32[]{:S(2)}) collective-permute-start(bf16[256,2048]{1,0:T(8,128)(2,1)S(1)} %get-tuple-element.114), channel_id=1, source_target_pairs={{0,2},{2,0},{4,6},{6,4},{8,10},{10,8},{12,14},{14,12},{16,18},{18,... | collective-permute-start | bytes 3145736 | tf_op jit(solution)/shard_map/ppermute | solution.py:279
  6.2 40.5 %collective-permute-start.2 = (bf16[256,2048]{1,0:T(8,128)(2,1)S(1)}, bf16[256,2048]{1,0:T(8,128)(2,1)}, u32[]{:S(2)}, u32[]{:S(2)}) collective-permute-start(bf16[256,2048]{1,0:T(8,128)(2,1)S(1)} %get-tuple-element.114), channel_id=1, source_target_pairs={{0,4},{2,6},{4,0},{6,2},{8,12},{10,14},{12,8},{14,10},{16,20},{18,... | collective-permute-start | bytes 3145736 | tf_op jit(solution)/shard_map/ppermute | solution.py:279
  9.5 28.4 %collective-permute-start.9 = (bf16[128,640]{1,0:T(8,128)(2,1)S(1)}, bf16[128,640]{1,0:T(8,128)(2,1)S(1)}, u32[]{:S(2)}, u32[]{:S(2)}) collective-permute-start(bf16[128,640]{1,0:T(8,128)(2,1)S(1)} %get-tuple-element.211), channel_id=1, source_target_pairs={{0,4},{2,6},{4,0},{6,2},{8,12},{10,14},{12,8},{14,10},{16,20},{18,... | collective-permute-start | bytes 491528 | tf_op jit(solution)/shard_map/ppermute | solution.py:279
  10.0 27.8 %collective-permute-start.10 = (bf16[128,640]{1,0:T(8,128)(2,1)S(1)}, bf16[128,640]{1,0:T(8,128)(2,1)S(1)}, u32[]{:S(2)}, u32[]{:S(2)}) collective-permute-start(bf16[128,640]{1,0:T(8,128)(2,1)S(1)} %get-tuple-element.212), channel_id=1, source_target_pairs={{0,6},{2,4},{4,2},{6,0},{8,14},{10,12},{12,10},{14,8},{16,22},{18,... | collective-permute-start | bytes 491528 | tf_op jit(solution)/shard_map/ppermute | solution.py:279
  30.3 31.1 %collective-permute-start.1 = (bf16[256,2048]{1,0:T(8,128)(2,1)}, bf16[256,2048]{1,0:T(8,128)(2,1)}, u32[]{:S(2)}, u32[]{:S(2)}) collective-permute-start(bf16[256,2048]{1,0:T(8,128)(2,1)} %collective-permute-done), channel_id=1, source_target_pairs={{0,1},{1,0},{2,3},{3,2},{4,5},{5,4},{6,7},{7,6},{8,9},{9,8},{10,11... | collective-permute-start | bytes 3145736 | tf_op jit(solution)/shard_map/ppermute | solution.py:282
  46.7 30.2 %collective-permute-start.3 = (bf16[256,2048]{1,0:T(8,128)(2,1)}, bf16[256,2048]{1,0:T(8,128)(2,1)S(1)}, u32[]{:S(2)}, u32[]{:S(2)}) collective-permute-start(bf16[256,2048]{1,0:T(8,128)(2,1)} %collective-permute-done.2), channel_id=1, source_target_pairs={{0,1},{1,0},{2,3},{3,2},{4,5},{5,4},{6,7},{7,6},{8,9},{9,8},{10,11... | collective-permute-start | bytes 3145736 | tf_op jit(solution)/shard_map/ppermute | solution.py:282
  69.9 99.7 %collective-permute-start.53 = (bf16[704,128]{1,0:T(8,128)(2,1)}, bf16[704,128]{1,0:T(8,128)(2,1)}, u32[]{:S(2)}, u32[]{:S(2)}) collective-permute-start(bf16[704,128]{1,0:T(8,128)(2,1)} %get-tuple-element.205), channel_id=1, source_target_pairs={{0,6},{2,4},{4,2},{6,0},{8,14},{10,12},{12,10},{14,8},{16,22},{18,... | collective-permute-start | bytes 540680 | tf_op jit(solution)/shard_map/ppermute | solution.py:279
  80.2 92.2 %collective-permute-start.51 = (bf16[704,128]{1,0:T(8,128)(2,1)}, bf16[704,128]{1,0:T(8,128)(2,1)}, u32[]{:S(2)}, u32[]{:S(2)}) collective-permute-start(bf16[704,128]{1,0:T(8,128)(2,1)} %get-tuple-element.206), channel_id=1, source_target_pairs={{0,2},{2,0},{4,6},{6,4},{8,10},{10,8},{12,14},{14,12},{16,18},{18,... | collective-permute-start | bytes 540680 | tf_op jit(solution)/shard_map/ppermute | solution.py:279
  145.0 29.0 %collective-permute-start.52 = (bf16[704,128]{1,0:T(8,128)(2,1)}, bf16[704,128]{1,0:T(8,128)(2,1)}, u32[]{:S(2)}, u32[]{:S(2)}) collective-permute-start(bf16[704,128]{1,0:T(8,128)(2,1)} %get-tuple-element.207), channel_id=1, source_target_pairs={{0,4},{2,6},{4,0},{6,2},{8,12},{10,14},{12,8},{14,10},{16,20},{18,... | collective-permute-start | bytes 540680 | tf_op jit(solution)/shard_map/ppermute | solution.py:279
  145.5 60.8 %collective-permute-start.34 = (bf16[256,2048]{1,0:T(8,128)(2,1)}, bf16[256,2048]{1,0:T(8,128)(2,1)}, u32[]{:S(2)}, u32[]{:S(2)}) collective-permute-start(bf16[256,2048]{1,0:T(8,128)(2,1)} %get-tuple-element.110), channel_id=1, source_target_pairs={{0,2},{2,0},{4,6},{6,4},{8,10},{10,8},{12,14},{14,12},{16,18},{18,... | collective-permute-start | bytes 3145736 | tf_op jit(solution)/shard_map/ppermute | solution.py:279
  162.2 116.3 %collective-permute-start.20 = (bf16[4,256,2048]{2,1,0:T(8,128)(2,1)}, bf16[4,256,2048]{2,1,0:T(8,128)(2,1)}, u32[]{:S(2)}, u32[]{:S(2)}) collective-permute-start(bf16[4,256,2048]{2,1,0:T(8,128)(2,1)} %get-tuple-element.34), channel_id=1, source_target_pairs={{0,1},{1,0},{2,3},{3,2},{4,5},{5,4},{6,7},{7,6},{8,9},{9,8},{10,11... | collective-permute-start | bytes 12582920 | tf_op jit(solution)/shard_map/ppermute | solution.py:282
  172.4 38.5 %collective-permute-start.36 = (bf16[256,2048]{1,0:T(8,128)(2,1)}, bf16[256,2048]{1,0:T(8,128)(2,1)}, u32[]{:S(2)}, u32[]{:S(2)}) collective-permute-start(bf16[256,2048]{1,0:T(8,128)(2,1)} %get-tuple-element.110), channel_id=1, source_target_pairs={{0,4},{2,6},{4,0},{6,2},{8,12},{10,14},{12,8},{14,10},{16,20},{18,... | collective-permute-start | bytes 3145736 | tf_op jit(solution)/shard_map/ppermute | solution.py:279
  191.5 30.7 %collective-permute-start.57 = (bf16[704,512]{1,0:T(8,128)(2,1)}, bf16[704,512]{1,0:T(8,128)(2,1)}, u32[]{:S(2)}, u32[]{:S(2)}) collective-permute-start(bf16[704,512]{1,0:T(8,128)(2,1)} %pad_maximum_fusion.6), channel_id=1, source_target_pairs={{8,0},{10,2},{12,4},{14,6},{16,8},{18,10},{20,12},{22,14},{24,16},... | collective-permute-start | bytes 2162696 | tf_op jit(solution)/shard_map/ppermute | solution.py:290
  198.6 27.2 %collective-permute-start.54 = (bf16[704,512]{1,0:T(8,128)(2,1)}, bf16[704,512]{1,0:T(8,128)(2,1)}, u32[]{:S(2)}, u32[]{:S(2)}) collective-permute-start(bf16[704,512]{1,0:T(8,128)(2,1)} %pad_maximum_fusion.6), channel_id=1, source_target_pairs={{0,8},{2,10},{4,12},{6,14},{8,16},{10,18},{12,20},{14,22},{16,24},... | collective-permute-start | bytes 2162696 | tf_op jit(solution)/shard_map/ppermute | solution.py:290
  222.2 55.0 %collective-permute-start.48 = (bf16[512,1408]{1,0:T(8,128)(2,1)}, bf16[512,1408]{1,0:T(8,128)(2,1)}, u32[]{:S(2)}, u32[]{:S(2)}) collective-permute-start(bf16[512,1408]{1,0:T(8,128)(2,1)} %pad_maximum_fusion.4), channel_id=1, source_target_pairs={{8,0},{10,2},{12,4},{14,6},{16,8},{18,10},{20,12},{22,14},{24,16},... | collective-permute-start | bytes 4325384 | tf_op jit(solution)/shard_map/ppermute | solution.py:290
  232.9 43.8 %collective-permute-start.58 = (bf16[704,512]{1,0:T(8,128)(2,1)}, bf16[704,512]{1,0:T(8,128)(2,1)S(1)}, u32[]{:S(2)}, u32[]{:S(2)}) collective-permute-start(bf16[704,512]{1,0:T(8,128)(2,1)} %collective-permute-done.57), channel_id=1, source_target_pairs={{8,0},{10,2},{12,4},{14,6},{16,8},{18,10},{20,12},{22,14},{9,1},{1... | collective-permute-start | bytes 2162696 | tf_op jit(solution)/shard_map/ppermute | solution.py:290
  234.2 42.5 %collective-permute-start.55 = (bf16[704,512]{1,0:T(8,128)(2,1)}, bf16[704,512]{1,0:T(8,128)(2,1)}, u32[]{:S(2)}, u32[]{:S(2)}) collective-permute-start(bf16[704,512]{1,0:T(8,128)(2,1)} %collective-permute-done.54), channel_id=1, source_target_pairs={{8,16},{10,18},{12,20},{14,22},{16,24},{18,26},{20,28},{22,30},{9,... | collective-permute-start | bytes 2162696 | tf_op jit(solution)/shard_map/ppermute | solution.py:290
  243.7 54.3 %collective-permute-start.45 = (bf16[512,1408]{1,0:T(8,128)(2,1)}, bf16[512,1408]{1,0:T(8,128)(2,1)}, u32[]{:S(2)}, u32[]{:S(2)}) collective-permute-start(bf16[512,1408]{1,0:T(8,128)(2,1)} %pad_maximum_fusion.4), channel_id=1, source_target_pairs={{0,8},{2,10},{4,12},{6,14},{8,16},{10,18},{12,20},{14,22},{16,24},... | collective-permute-start | bytes 4325384 | tf_op jit(solution)/shard_map/ppermute | solution.py:290
  297.9 36.4 %collective-permute-start.49 = (bf16[512,1408]{1,0:T(8,128)(2,1)}, bf16[512,1408]{1,0:T(8,128)(2,1)S(1)}, u32[]{:S(2)}, u32[]{:S(2)}) collective-permute-start(bf16[512,1408]{1,0:T(8,128)(2,1)} %collective-permute-done.48), channel_id=1, source_target_pairs={{8,0},{10,2},{12,4},{14,6},{16,8},{18,10},{20,12},{22,14},{9,1},{1... | collective-permute-start | bytes 4325384 | tf_op jit(solution)/shard_map/ppermute | solution.py:290
  299.2 36.3 %collective-permute-start.46 = (bf16[512,1408]{1,0:T(8,128)(2,1)}, bf16[512,1408]{1,0:T(8,128)(2,1)S(1)}, u32[]{:S(2)}, u32[]{:S(2)}) collective-permute-start(bf16[512,1408]{1,0:T(8,128)(2,1)} %collective-permute-done.45), channel_id=1, source_target_pairs={{8,16},{10,18},{12,20},{14,22},{16,24},{18,26},{20,28},{22,30},{9,... | collective-permute-start | bytes 4325384 | tf_op jit(solution)/shard_map/ppermute | solution.py:290
  334.3 33.8 %collective-permute-start.50 = (bf16[512,1408]{1,0:T(8,128)(2,1)S(1)}, bf16[512,1408]{1,0:T(8,128)(2,1)S(1)}, u32[]{:S(2)}, u32[]{:S(2)}) collective-permute-start(bf16[512,1408]{1,0:T(8,128)(2,1)S(1)} %collective-permute-done.49), channel_id=1, source_target_pairs={{8,0},{10,2},{12,4},{14,6},{9,1},{11,3},{13,5},{15,7}} | collective-permute-start | bytes 4325384 | tf_op jit(solution)/shard_map/ppermute | solution.py:290
  335.6 37.3 %collective-permute-start.47 = (bf16[512,1408]{1,0:T(8,128)(2,1)S(1)}, bf16[512,1408]{1,0:T(8,128)(2,1)S(1)}, u32[]{:S(2)}, u32[]{:S(2)}) collective-permute-start(bf16[512,1408]{1,0:T(8,128)(2,1)S(1)} %collective-permute-done.46), channel_id=1, source_target_pairs={{16,24},{18,26},{20,28},{22,30},{17,25},{19,27},{21,29},{23,31}} | collective-permute-start | bytes 4325384 | tf_op jit(solution)/shard_map/ppermute | solution.py:290
  338.6 39.0 %collective-permute-start.28 = (bf16[256,2048]{1,0:T(8,128)(2,1)S(1)}, bf16[256,2048]{1,0:T(8,128)(2,1)S(1)}, u32[]{:S(2)}, u32[]{:S(2)}) collective-permute-start(bf16[256,2048]{1,0:T(8,128)(2,1)S(1)} %get-tuple-element.112), channel_id=1, source_target_pairs={{0,4},{2,6},{4,0},{6,2},{8,12},{10,14},{12,8},{14,10},{16,20},{18,... | collective-permute-start | bytes 3145736 | tf_op jit(solution)/shard_map/ppermute | solution.py:279
  339.2 39.1 %collective-permute-start.26 = (bf16[256,2048]{1,0:T(8,128)(2,1)S(1)}, bf16[256,2048]{1,0:T(8,128)(2,1)S(1)}, u32[]{:S(2)}, u32[]{:S(2)}) collective-permute-start(bf16[256,2048]{1,0:T(8,128)(2,1)S(1)} %get-tuple-element.112), channel_id=1, source_target_pairs={{0,2},{2,0},{4,6},{6,4},{8,10},{10,8},{12,14},{14,12},{16,18},{18,... | collective-permute-start | bytes 3145736 | tf_op jit(solution)/shard_map/ppermute | solution.py:279
  392.9 154.0 %collective-permute-start.125 = (f32[2,128]{1,0:T(2,128)S(1)}, f32[2,128]{1,0:T(2,128)S(1)}, u32[]{:S(2)}, u32[]{:S(2)}) collective-permute-start(f32[2,128]{1,0:T(2,128)S(1)} %max.66), channel_id=1, source_target_pairs={{0,24},{2,26},{4,28},{6,30},{1,25},{3,27},{5,29},{7,31}} | collective-permute-start | bytes 3080 | tf_op jit(solution)/shard_map/ppermute | solution.py:290
  400.5 147.7 %collective-permute-start.124 = (f32[2,128]{1,0:T(2,128)S(1)}, f32[2,128]{1,0:T(2,128)S(1)}, u32[]{:S(2)}, u32[]{:S(2)}) collective-permute-start(f32[2,128]{1,0:T(2,128)S(1)} %max.66), channel_id=1, source_target_pairs={{16,0},{18,2},{20,4},{22,6},{24,8},{26,10},{28,12},{30,14},{17,1},... | collective-permute-start | bytes 3080 | tf_op jit(solution)/shard_map/ppermute | solution.py:290
  488.2 54.5 %collective-permute-start.99 = (bf16[512,1408]{1,0:T(8,128)(2,1)}, bf16[512,1408]{1,0:T(8,128)(2,1)}, u32[]{:S(2)}, u32[]{:S(2)}) collective-permute-start(bf16[512,1408]{1,0:T(8,128)(2,1)} %get-tuple-element.141), channel_id=1, source_target_pairs={{0,8},{2,10},{4,12},{6,14},{1,9},{3,11},{5,13},{7,15}} | collective-permute-start | bytes 4325384 | tf_op jit(solution)/shard_map/ppermute | solution.py:290
  491.7 44.9 %collective-permute-start.110 = (bf16[704,512]{1,0:T(8,128)(2,1)}, bf16[704,512]{1,0:T(8,128)(2,1)}, u32[]{:S(2)}, u32[]{:S(2)}) collective-permute-start(bf16[704,512]{1,0:T(8,128)(2,1)} %add_convert_fusion.9), channel_id=1, source_target_pairs={{0,8},{2,10},{4,12},{6,14},{8,16},{10,18},{12,20},{14,22},{1,9},{3... | collective-permute-start | bytes 2162696 | tf_op jit(solution)/shard_map/ppermute | solution.py:290
  502.6 50.5 %collective-permute-start.123 = (f32[2,128]{1,0:T(2,128)S(1)}, f32[2,128]{1,0:T(2,128)S(1)}, u32[]{:S(2)}, u32[]{:S(2)}) collective-permute-start(f32[2,128]{1,0:T(2,128)S(1)} %max.66), channel_id=1, source_target_pairs={{0,16},{2,18},{4,20},{6,22},{8,24},{10,26},{12,28},{14,30},{1,17},... | collective-permute-start | bytes 3080 | tf_op jit(solution)/shard_map/ppermute | solution.py:290
  553.2 67.4 %collective-permute-start.102 = (bf16[512,1408]{1,0:T(8,128)(2,1)}, bf16[512,1408]{1,0:T(8,128)(2,1)}, u32[]{:S(2)}, u32[]{:S(2)}) collective-permute-start(bf16[512,1408]{1,0:T(8,128)(2,1)} %get-tuple-element.142), channel_id=1, source_target_pairs={{24,16},{26,18},{28,20},{30,22},{25,17},{27,19},{29,21},{31,23}} | collective-permute-start | bytes 4325384 | tf_op jit(solution)/shard_map/ppermute | solution.py:290
  555.0 81.9 %collective-permute-start.60 = (bf16[4,256,2048]{2,1,0:T(8,128)(2,1)}, bf16[4,256,2048]{2,1,0:T(8,128)(2,1)}, u32[]{:S(2)}, u32[]{:S(2)}) collective-permute-start(bf16[4,256,2048]{2,1,0:T(8,128)(2,1)} %slice_bitcast_fusion), channel_id=1, source_target_pairs={{0,1},{1,0},{2,3},{3,2},{4,5},{5,4},{6,7},{7,6},{8,9},{9,8},{10,11... | collective-permute-start | bytes 12582920 | tf_op jit(solution)/shard_map/ppermute | solution.py:282
  555.0 67.1 %collective-permute-start.100 = (bf16[512,1408]{1,0:T(8,128)(2,1)}, bf16[512,1408]{1,0:T(8,128)(2,1)}, u32[]{:S(2)}, u32[]{:S(2)}) collective-permute-start(bf16[512,1408]{1,0:T(8,128)(2,1)} %add_convert_fusion.4), channel_id=1, source_target_pairs={{0,8},{2,10},{4,12},{6,14},{8,16},{10,18},{12,20},{14,22},{1,9},{3... | collective-permute-start | bytes 4325384 | tf_op jit(solution)/shard_map/ppermute | solution.py:290
  565.6 45.0 %collective-permute-start.111 = (bf16[704,512]{1,0:T(8,128)(2,1)}, bf16[704,512]{1,0:T(8,128)(2,1)}, u32[]{:S(2)}, u32[]{:S(2)}) collective-permute-start(bf16[704,512]{1,0:T(8,128)(2,1)} %get-tuple-element.151), channel_id=1, source_target_pairs={{0,8},{2,10},{4,12},{6,14},{8,16},{10,18},{12,20},{14,22},{16,24},... | collective-permute-start | bytes 2162696 | tf_op jit(solution)/shard_map/ppermute | solution.py:290
  567.8 43.5 %collective-permute-start.114 = (bf16[704,512]{1,0:T(8,128)(2,1)}, bf16[704,512]{1,0:T(8,128)(2,1)}, u32[]{:S(2)}, u32[]{:S(2)}) collective-permute-start(bf16[704,512]{1,0:T(8,128)(2,1)} %add_convert_fusion.6), channel_id=1, source_target_pairs={{8,0},{10,2},{12,4},{14,6},{16,8},{18,10},{20,12},{22,14},{24,16},... | collective-permute-start | bytes 2162696 | tf_op jit(solution)/shard_map/ppermute | solution.py:290
  610.7 40.2 %collective-permute-start.66 = (bf16[4,256,2048]{2,1,0:T(8,128)(2,1)}, bf16[4,256,2048]{2,1,0:T(8,128)(2,1)}, u32[]{:S(2)}, u32[]{:S(2)}) collective-permute-start(bf16[4,256,2048]{2,1,0:T(8,128)(2,1)} %get-tuple-element.37), channel_id=1, source_target_pairs={{0,1},{1,0},{2,3},{3,2},{4,5},{5,4},{6,7},{7,6},{8,9},{9,8},{10,11... | collective-permute-start | bytes 12582920 | tf_op jit(solution)/shard_map/ppermute | solution.py:282
  628.5 94.2 %collective-permute-start.101 = (bf16[512,1408]{1,0:T(8,128)(2,1)}, bf16[512,1408]{1,0:T(8,128)(2,1)}, u32[]{:S(2)}, u32[]{:S(2)}) collective-permute-start(bf16[512,1408]{1,0:T(8,128)(2,1)} %get-tuple-element.139), channel_id=1, source_target_pairs={{0,8},{2,10},{4,12},{6,14},{8,16},{10,18},{12,20},{14,22},{16,24},... | collective-permute-start | bytes 4325384 | tf_op jit(solution)/shard_map/ppermute | solution.py:290
  634.0 32.3 %collective-permute-start.103 = (bf16[512,1408]{1,0:T(8,128)(2,1)}, bf16[512,1408]{1,0:T(8,128)(2,1)}, u32[]{:S(2)}, u32[]{:S(2)}) collective-permute-start(bf16[512,1408]{1,0:T(8,128)(2,1)} %get-tuple-element.140), channel_id=1, source_target_pairs={{16,8},{18,10},{20,12},{22,14},{24,16},{26,18},{28,20},{30,22},{17... | collective-permute-start | bytes 4325384 | tf_op jit(solution)/shard_map/ppermute | solution.py:290
  650.4 29.0 %collective-permute-start.63 = (bf16[2,128,2048]{2,1,0:T(8,128)(2,1)}, bf16[2,128,2048]{2,1,0:T(8,128)(2,1)}, u32[]{:S(2)}, u32[]{:S(2)}) collective-permute-start(bf16[2,128,2048]{2,1,0:T(8,128)(2,1)} %slice.502), channel_id=1, source_target_pairs={{0,4},{2,6},{4,0},{6,2},{8,12},{10,14},{12,8},{14,10},{16,20},{18,... | collective-permute-start | bytes 3145736 | tf_op jit(solution)/shard_map/ppermute | solution.py:279
  664.8 32.3 %collective-permute-start.67 = (bf16[2,128,2048]{2,1,0:T(8,128)(2,1)S(1)}, bf16[2,128,2048]{2,1,0:T(8,128)(2,1)S(1)}, u32[]{:S(2)}, u32[]{:S(2)}) collective-permute-start(bf16[2,128,2048]{2,1,0:T(8,128)(2,1)S(1)} %slice.408), channel_id=1, source_target_pairs={{0,2},{2,0},{4,6},{6,4},{8,10},{10,8},{12,14},{14,12},{16,18},{18,... | collective-permute-start | bytes 3145736 | tf_op jit(solution)/shard_map/ppermute | solution.py:279
  666.3 32.9 %collective-permute-start.69 = (bf16[2,128,2048]{2,1,0:T(8,128)(2,1)S(1)}, bf16[2,128,2048]{2,1,0:T(8,128)(2,1)S(1)}, u32[]{:S(2)}, u32[]{:S(2)}) collective-permute-start(bf16[2,128,2048]{2,1,0:T(8,128)(2,1)S(1)} %slice.512), channel_id=1, source_target_pairs={{0,4},{2,6},{4,0},{6,2},{8,12},{10,14},{12,8},{14,10},{16,20},{18,... | collective-permute-start | bytes 3145736 | tf_op jit(solution)/shard_map/ppermute | solution.py:279
  676.3 46.4 %collective-permute-start.104 = (bf16[512,1408]{1,0:T(8,128)(2,1)S(1)}, bf16[512,1408]{1,0:T(8,128)(2,1)S(1)}, u32[]{:S(2)}, u32[]{:S(2)}) collective-permute-start(bf16[512,1408]{1,0:T(8,128)(2,1)S(1)} %add_convert_fusion.1), channel_id=1, source_target_pairs={{8,0},{10,2},{12,4},{14,6},{16,8},{18,10},{20,12},{22,14},{24,16},... | collective-permute-start | bytes 4325384 | tf_op jit(solution)/shard_map/ppermute | solution.py:290
  681.2 29.2 %collective-permute-start.62 = (bf16[128,2048]{1,0:T(8,128)(2,1)S(1)}, bf16[128,2048]{1,0:T(8,128)(2,1)S(1)}, u32[]{:S(2)}, u32[]{:S(2)}) collective-permute-start(bf16[128,2048]{1,0:T(8,128)(2,1)S(1)} %get-tuple-element.131), channel_id=1, source_target_pairs={{0,4},{2,6},{4,0},{6,2},{8,12},{10,14},{12,8},{14,10},{16,20},{18,... | collective-permute-start | bytes 1572872 | tf_op jit(solution)/shard_map/ppermute | solution.py:279
  732.4 30.7 %collective-permute-start.73 = (bf16[256,2048]{1,0:T(8,128)(2,1)S(1)}, bf16[256,2048]{1,0:T(8,128)(2,1)S(1)}, u32[]{:S(2)}, u32[]{:S(2)}) collective-permute-start(bf16[256,2048]{1,0:T(8,128)(2,1)S(1)} %get-tuple-element.105), channel_id=1, source_target_pairs={{0,2},{2,0},{4,6},{6,4},{8,10},{10,8},{12,14},{14,12},{16,18},{18,... | collective-permute-start | bytes 3145736 | tf_op jit(solution)/shard_map/ppermute | solution.py:279
  735.1 29.4 %collective-permute-start.75 = (bf16[256,2048]{1,0:T(8,128)(2,1)S(1)}, bf16[256,2048]{1,0:T(8,128)(2,1)S(1)}, u32[]{:S(2)}, u32[]{:S(2)}) collective-permute-start(bf16[256,2048]{1,0:T(8,128)(2,1)S(1)} %get-tuple-element.105), channel_id=1, source_target_pairs={{0,4},{2,6},{4,0},{6,2},{8,12},{10,14},{12,8},{14,10},{16,20},{18,... | collective-permute-start | bytes 3145736 | tf_op jit(solution)/shard_map/ppermute | solution.py:279
  737.5 31.0 %collective-permute-start.72 = (bf16[256,2048]{1,0:T(8,128)(2,1)S(1)}, bf16[256,2048]{1,0:T(8,128)(2,1)S(1)}, u32[]{:S(2)}, u32[]{:S(2)}) collective-permute-start(bf16[256,2048]{1,0:T(8,128)(2,1)S(1)} %get-tuple-element.105), channel_id=1, source_target_pairs={{0,1},{1,0},{2,3},{3,2},{4,5},{5,4},{6,7},{7,6},{8,9},{9,8},{10,11... | collective-permute-start | bytes 3145736 | tf_op jit(solution)/shard_map/ppermute | solution.py:282
  768.5 133.9 %collective-permute-start.65 = (bf16[256,2048]{1,0:T(8,128)(2,1)}, bf16[256,2048]{1,0:T(8,128)(2,1)}, u32[]{:S(2)}, u32[]{:S(2)}) collective-permute-start(bf16[256,2048]{1,0:T(8,128)(2,1)} %get-tuple-element.150), channel_id=1, source_target_pairs={{0,1},{1,0},{2,3},{3,2},{4,5},{5,4},{6,7},{7,6},{8,9},{9,8},{10,11... | collective-permute-start | bytes 3145736 | tf_op jit(solution)/shard_map/ppermute | solution.py:282
  779.0 144.3 %collective-permute-start.71 = (f32[256,2048]{1,0:T(8,128)}, f32[256,2048]{1,0:T(8,128)}, u32[]{:S(2)}, u32[]{:S(2)}) collective-permute-start(f32[256,2048]{1,0:T(8,128)} %get-tuple-element.106), channel_id=1, source_target_pairs={{0,1},{1,0},{2,3},{3,2},{4,5},{5,4},{6,7},{7,6},{8,9},{9,8},{10,11... | collective-permute-start | bytes 6291464 | tf_op jit(solution)/shard_map/ppermute | solution.py:282
  860.4 68.3 %collective-permute-start.84 = (bf16[4,256,2048]{2,1,0:T(8,128)(2,1)}, bf16[4,256,2048]{2,1,0:T(8,128)(2,1)}, u32[]{:S(2)}, u32[]{:S(2)}) collective-permute-start(bf16[4,256,2048]{2,1,0:T(8,128)(2,1)} %get-tuple-element.44), channel_id=1, source_target_pairs={{0,1},{1,0},{2,3},{3,2},{4,5},{5,4},{6,7},{7,6},{8,9},{9,8},{10,11... | collective-permute-start | bytes 12582920 | tf_op jit(solution)/shard_map/ppermute | solution.py:282
  (166 other events, 2372.6 us)

commit v2 on v1

--- a/solution.py
+++ b/solution.py
@@ -160,12 +160,51 @@
         out0[0] = part
 
 
-def mlp_kernel(n_ref, cot_ref, wgu_ref, wd_ref, h_ref, ggu_ref, out1, out0):
+def line_blocks(z, top, near, far, slab):
+    found = [(None, z, near[0])]
+    for k in range(1, top):
+        for sign in (-1, 1):
+            at = z + sign * k
+            i = 2 * k - (sign < 0)
+            src = near[i] if i < len(near) else rows_of(far, jnp.clip(at, 0, top - 1), slab)
+            found.append(((at >= 0) & (at < top), at, src))
+    return found
+
+
+def mlp_kernel(
+    top, n_ref, cot_ref, g0, gu1, gd1, gu2, gd2, g_far, d0, du1, dd1, d_far,
+    h_ref, ggu_ref, out1, out0, dw_out, wgu_ref, wd_ref, sems, out_sem,
+):
     g = pl.program_id(0)
     half = pl.num_programs(0) // 2
+    slab = g0.shape[0]
+    z = lax.div(lax.axis_index("seq"), PLANE)
+
+    @pl.when(g == 0)
+    def _():
+        copies = []
+        for ref, near, far in ((wgu_ref, (g0, gu1, gd1, gu2, gd2), g_far), (wd_ref, (d0, du1, dd1), d_far)):
+            for cond, block, src in line_blocks(z, top, near, far, slab):
+
+                def copy(ref=ref, block=block, src=src, i=len(copies)):
+                    return pltpu.make_async_copy(src, rows_of(ref, block, slab), sems.at[i])
+
+                copies.append((cond, copy))
+        for what in ("start", "wait"):
+            for cond, copy in copies:
+                if cond is None:
+                    getattr(copy(), what)()
+                else:
+                    pl.when(cond)(lambda copy=copy: getattr(copy(), what)())
+        pltpu.make_async_copy(wd_ref, dw_out, out_sem.at[0]).start()
+
+    @pl.when(g == 2 * half - 1)
+    def _():
+        pltpu.make_async_copy(wd_ref, dw_out, out_sem.at[0]).wait()
+
     main = (wgu_ref.shape[1] - 128) // 2
     gu = dot(n_ref[0], wgu_ref[...])
-    gh = dot(cot_ref[0], wd_ref[...], NT)
+    gh = dot(cot_ref[0], wd_ref[...])
 
     def parts(gate, up, grad):
         sig = 1.0 / (1.0 + jnp.exp(-gate))
@@ -345,6 +384,575 @@
         )
 
 
+MESH = pl.DeviceIdType.MESH
+N_SEMS = 160
+
+
+def for_rows(count, body, block=32):
+    def step(i, _):
+        body(pl.ds(pl.multiple_of(i * block, block), block))
+        return 0
+
+    lax.fori_loop(0, count // block, step, 0)
+
+
+class Copies:
+    def __init__(self, items):
+        self.items = items
+
+    def each(self, what, conditions):
+        for (copy, *_), cond in zip(self.items, conditions):
+            if cond is None:
+                getattr(copy(), what)()
+            else:
+
+                @pl.when(cond)
+                def _(copy=copy):
+                    getattr(copy(), what)()
+
+    def start(self):
+        self.each("start", [i[1] for i in self.items])
+        return self
+
+    def wait_send(self):
+        self.each("wait_send", [i[1] for i in self.items])
+
+    def wait_recv(self):
+        self.each("wait_recv", [i[2] for i in self.items])
+
+
+class Net:
+    def __init__(self, n, sends, recvs, locals_):
+        self.n, self.top = n, n // PLANE
+        self.sends, self.recvs, self.locals_ = sends, recvs, locals_
+        self.k = self.l = 0
+        self.sent, self.local = [], []
+        s, c = lax.axis_index("seq"), lax.axis_index("head")
+        self.s, self.c = s, c
+        self.z, self.p = lax.div(s, PLANE), lax.rem(s, PLANE)
+        p = self.p
+        self.part = [p, p + 1 - 2 * lax.rem(p, 2), p + 2 - 4 * lax.div(p, 2), 3 - p]
+        base = s - p
+        self.X, self.Y, self.D = ({"seq": base + q} for q in self.part[1:])
+        self.C = {"head": 1 - c}
+        self.up, self.down = {"seq": s + PLANE}, {"seq": s - PLANE}
+        self.has_up, self.has_down = self.z < self.top - 1, self.z > 0
+
+    def barrier(self, partners, line=False):
+        sem = pltpu.get_barrier_semaphore()
+        for to in partners:
+            pl.semaphore_signal(sem, inc=1, device_id=to, device_id_type=MESH)
+        count = len(partners)
+        if line:
+            for cond, to in ((self.has_up, self.up), (self.has_down, self.down)):
+
+                @pl.when(cond)
+                def _(to=to):
+                    pl.semaphore_signal(sem, inc=1, device_id=to, device_id_type=MESH)
+
+            count = count + self.has_up.astype(jnp.int32) + self.has_down.astype(jnp.int32)
+        pl.semaphore_wait(sem, count)
+
+    def barrier_hops(self, hops, back):
+        sem = pltpu.get_barrier_semaphore()
+        for hop in hops:
+            for sign in (1, -1):
+                at = self.z + sign * hop
+
+                @pl.when((at >= 0) & (at < self.top))
+                def _(sign=sign, hop=hop):
+                    to = {"seq": self.s + sign * hop * PLANE}
+                    pl.semaphore_signal(sem, inc=1, device_id=to, device_id_type=MESH)
+
+        pl.semaphore_wait(sem, self.top - 1)
+
+    def remote(self, src, dst, to, when=None, arrives=None):
+        i = self.k
+        self.k += 1
+        assert i < N_SEMS
+
+        def copy():
+            return pltpu.make_async_remote_copy(
+                src_ref=src(),
+                dst_ref=dst(),
+                send_sem=self.sends.at[i],
+                recv_sem=self.recvs.at[i],
+                device_id=to,
+                device_id_type=MESH,
+            )
+
+        made = Copies([(copy, when, arrives)])
+        self.sent.append(made)
+        return made
+
+    def put(self, src, dst, when=None):
+        i = self.l
+        self.l += 1
+        assert i < N_SEMS
+
+        def copy():
+            return pltpu.make_async_copy(src(), dst(), self.locals_.at[i])
+
+        class Local(Copies):
+            def wait(self):
+                self.each("wait", [when])
+
+        made = Local([(copy, when, when)])
+        made.start()
+        self.local.append(made)
+        return made
+
+    def finish(self):
+        for made in self.sent:
+            made.wait_send()
+
+    def step(self, k, src_up, src_down, dst_up, dst_down):
+        z, top = self.z, self.top
+        up = self.remote(src_up, dst_up, self.up, (z >= k - 1) & self.has_up, z >= k)
+        down = self.remote(src_down, dst_down, self.down, (z + k <= top) & self.has_down, z + k <= top - 1)
+        return Copies(up.items + down.items)
+
+
+def rows_of(ref, block, rows):
+    return ref.at[pl.ds(pl.multiple_of(block * rows, 16), rows)]
+
+
+class Reduce:
+    def scratch(slots, rows, width):
+        cut = rows // 2
+        return [
+            pltpu.VMEM((slots, rows, width), BF),
+            pltpu.VMEM((slots, rows, width), BF),
+            pltpu.VMEM((2, cut, width), BF),
+            pltpu.VMEM((2, cut, width), BF),
+            pltpu.VMEM((2, cut, width), BF),
+        ]
+
+    def __init__(self, net, p1, p0, own, rc, rx, ry, r2):
+        self.net, self.p1, self.p0 = net, p1, p0
+        self.own, self.rc, self.rx, self.ry, self.r2 = own, rc, rx, ry, r2
+        self.cut = rc.shape[1] // 2
+
+    def piece(self, ref, j, hf):
+        return ref.at[j, pl.ds(hf * self.cut, self.cut)]
+
+    def send_core(self):
+        net = self.net
+        self.load = net.put(lambda: self.p0, lambda: self.own)
+        self.core = {}
+        for j, hf in ((3, 0), (3, 1), (1, 0), (2, 1), (2, 0), (1, 1), (0, 0), (0, 1)):
+            self.core[j, hf] = net.remote(
+                functools.partial(self.piece, self.p1, j, hf), functools.partial(self.piece, self.rc, j, hf), net.C
+            ).start()
+        self.load.wait()
+
+    def add(self, j, hf):
+        self.core[j, hf].wait_recv()
+        rc, own = self.piece(self.rc, j, hf), self.piece(self.own, j, hf)
+
+        def body(r):
+            rc[r] = (rc[r].astype(F32) + own[r].astype(F32)).astype(BF)
+
+        for_rows(self.cut, body)
+
+    def first(self):
+        net, made = self.net, {}
+        for name, j, hf, land, to in (
+            ("x1", 3, 0, self.rx.at[1], net.X),
+            ("y1", 3, 1, self.ry.at[1], net.Y),
+            ("x0", 1, 0, self.rx.at[0], net.X),
+            ("y0", 2, 1, self.ry.at[0], net.Y),
+        ):
+            self.add(j, hf)
+            made[name] = net.remote(functools.partial(self.piece, self.rc, j, hf), lambda land=land: land, to).start()
+        self.made = made
+        for j, hf in ((2, 0), (1, 1), (0, 0), (0, 1)):
+            self.add(j, hf)
+
+    def second(self):
+        net = self.net
+        for name, j, hf, land, i, to in (("x1", 2, 0, self.rx, 0, net.Y), ("y1", 1, 1, self.ry, 1, net.X)):
+            self.made[name].wait_recv()
+            at = self.piece(self.rc, j, hf)
+
+            def body(r):
+                at[r] = (at[r].astype(F32) + land[1, r].astype(F32)).astype(BF)
+
+            for_rows(self.cut, body)
+            self.made["last", hf] = net.remote(
+                functools.partial(self.piece, self.rc, j, hf), lambda i=i: self.r2.at[i], to
+            ).start()
+
+    def last(self, hf, body):
+        self.made["x0" if hf == 0 else "y0"].wait_recv()
+        self.made["last", hf].wait_recv()
+        land = self.rx if hf == 0 else self.ry
+
+        def step(i, _):
+            r = pl.ds(pl.multiple_of(i * 32, 32), 32)
+            at = pl.ds(pl.multiple_of(hf * self.cut + i * 32, 32), 32)
+            total = self.rc[0, at].astype(F32) + land[0, r].astype(F32) + self.r2[hf, r].astype(F32)
+            body(at, total)
+            return 0
+
+        lax.fori_loop(0, self.cut // 32, step, 0)
+
+
+class Gather:
+    def __init__(self, net, out, rows):
+        self.net, self.out, self.rows, self.cut = net, out, rows, rows // 2
+
+    def half(self, ref, slot, hf):
+        return ref.at[slot, pl.ds(hf * self.cut, self.cut)]
+
+    def pass_on(self, src, slot, hf, to):
+        return self.net.remote(src, functools.partial(self.half, self.out, slot, hf), to).start()
+
+    def send(self, hf, src):
+        to, slot = (self.net.Y, 4) if hf == 0 else (self.net.X, 2)
+        setattr(self, f"on{hf}", self.pass_on(src, slot, hf, to))
+
+    def send_rest(self, srcs, core=True):
+        net = self.net
+        self.late = [self.pass_on(srcs[0], 2, 0, net.X), self.pass_on(srcs[1], 4, 1, net.Y)]
+        self.core = [self.pass_on(srcs[hf], 1, hf, net.C) for hf in (0, 1)] if core else []
+
+    def forward(self):
+        net, out = self.net, self.out
+        at = lambda slot, hf: functools.partial(self.half, out, slot, hf)
+        self.on0.wait_recv()
+        self.far = [self.pass_on(at(4, 0), 6, 0, net.X)]
+        self.on1.wait_recv()
+        self.far.append(self.pass_on(at(2, 1), 6, 1, net.Y))
+        self.core.append(self.pass_on(at(4, 0), 5, 0, net.C))
+        self.core.append(self.pass_on(at(2, 1), 3, 1, net.C))
+
+    def across(self):
+        net, out = self.net, self.out
+        at = lambda slot, hf: functools.partial(self.half, out, slot, hf)
+        self.late[0].wait_recv()
+        self.core.append(self.pass_on(at(2, 0), 3, 0, net.C))
+        self.late[1].wait_recv()
+        self.core.append(self.pass_on(at(4, 1), 5, 1, net.C))
+
+    def finish(self):
+        net, out = self.net, self.out
+        at = lambda slot, hf: functools.partial(self.half, out, slot, hf)
+        for hf in (0, 1):
+            self.far[hf].wait_recv()
+            self.core.append(self.pass_on(at(6, hf), 7, hf, net.C))
+        for copy in self.core:
+            copy.wait_recv()
+
+
+class ToParts:
+    def __init__(self, net, pack, rows):
+        self.own = net.put(lambda: pack.at[net.p], lambda: rows(net.p))
+        self.sent = [
+            net.remote(functools.partial(lambda j: pack.at[net.part[j]], j), lambda: rows(net.p), to).start()
+            for j, to in ((1, net.X), (2, net.Y), (3, net.D))
+        ]
+
+    def wait(self):
+        self.own.wait()
+        for copy in self.sent:
+            copy.wait_recv()
+
+
+def start_kernel(n, x, ap, gp, dp, x_all, aw, g0, g_up, g_down, d0, sends, recvs, locals_):
+    net = Net(n, sends, recvs, locals_)
+    z, c, top = net.z, net.c, net.top
+    db = ap.shape[1]
+    slab = PLANE * db
+    half = x.shape[0] // 2
+    cut = half // 2
+    net.barrier((net.X, net.Y, net.D, net.C), line=True)
+    attn = ToParts(net, ap, lambda q: rows_of(aw, z * PLANE + q, db))
+    gate_up = ToParts(net, gp, lambda q: rows_of(g0, q, db))
+    gather = Gather(net, x_all, half)
+    mine = lambda hf: functools.partial(rows_of, x, c * 2 + hf, cut)
+    net.put(lambda: rows_of(x, c, half), lambda: x_all.at[0])
+    net.put(lambda: rows_of(x, 1 - c, half), lambda: x_all.at[1])
+    gather.send(0, mine(0))
+    gather.send(1, mine(1))
+    gather.send_rest([mine(0), mine(1)], core=False)
+    attn.wait()
+
+    def attn_step(k):
+        up, down = (lambda: rows_of(aw, z - k + 1, slab)), (lambda: rows_of(aw, z + k - 1, slab))
+        return net.step(k, up, down, up, down).start()
+
+    line = attn_step(1)
+    gather.forward()
+    down_part = ToParts(net, dp, lambda q: rows_of(d0, q, db))
+    for k in range(2, top):
+        line.wait_recv()
+        line = attn_step(k)
+        if k == 2:
+            gather.across()
+    gate_up.wait()
+    gu = net.step(1, lambda: g0, lambda: g0, lambda: g_up, lambda: g_down).start()
+    line.wait_recv()
+    gather.finish()
+    down_part.wait()
+    gu.wait_recv()
+    for made in net.local[1:]:
+        if made not in (attn.own, gate_up.own, down_part.own):
+            made.wait()
+    net.finish()
+
+
+def norm_kernel(
+    n, p1, p0, x_ref, gain_ref, gu2, gd2, du1, dd1, cot, cx, cy, ca, cb,
+    out, resid_ref, gw, dw, cot_all, own, rc, rx, ry, r2, mine, sends, recvs, locals_,
+):
+    net = Net(n, sends, recvs, locals_)
+    z, c, top = net.z, net.c, net.top
+    slab = gu2.shape[0]
+    net.barrier((net.X, net.Y, net.C), line=True)
+    red = Reduce(net, p1, p0, own, rc, rx, ry, r2)
+    red.send_core()
+    half, cut = rc.shape[1], red.cut
+
+    gu_line = net.step(3, lambda: gu2, lambda: gd2, lambda: rows_of(gw, z - 2, slab), lambda: rows_of(gw, z + 2, slab))
+    gu_line.start()
+    d_line = net.step(2, lambda: du1, lambda: dd1, lambda: rows_of(dw, z - 1, slab), lambda: rows_of(dw, z + 1, slab))
+    d_line.start()
+    red.first()
+    kept = [
+        net.put(lambda: rows_of(cot, c, half), lambda: cot_all.at[0]),
+        net.put(lambda: rows_of(cot, 1 - c, half), lambda: cot_all.at[1]),
+        net.put(lambda: cx, lambda: cot_all.at[2]),
+        net.put(lambda: cy, lambda: cot_all.at[4]),
+        net.put(lambda: ca, lambda: cot_all.at[6, pl.ds(0, cut)]),
+        net.put(lambda: cb, lambda: cot_all.at[6, pl.ds(cut, cut)]),
+    ]
+    crossing = [
+        net.remote(lambda: cx, lambda: cot_all.at[3], net.C).start(),
+        net.remote(lambda: cy, lambda: cot_all.at[5], net.C).start(),
+        net.remote(lambda: ca, lambda: cot_all.at[7, pl.ds(0, cut)], net.C).start(),
+        net.remote(lambda: cb, lambda: cot_all.at[7, pl.ds(cut, cut)], net.C).start(),
+    ]
+    red.second()
+
+    def norm(at, total):
+        resid = x_ref[at].astype(F32) + total
+        resid_ref[at] = resid
+        inv = lax.rsqrt(jnp.mean(resid * resid, axis=-1, keepdims=True) + 1e-05)
+        mine[at] = (resid * inv * gain_ref[...]).astype(BF)
+
+    gather = Gather(net, out, half)
+    part = lambda hf: functools.partial(rows_of, mine, hf, cut)
+    for hf in (0, 1):
+        red.last(hf, norm)
+        gather.send(hf, part(hf))
+    gather.send_rest([part(0), part(1)])
+    kept.append(net.put(lambda: mine, lambda: out.at[0]))
+
+    def gu_step(k):
+        up, down = (lambda: rows_of(gw, z - k + 1, slab)), (lambda: rows_of(gw, z + k - 1, slab))
+        return net.step(k, up, down, up, down).start()
+
+    def d_step(k):
+        up, down = (lambda: rows_of(dw, z - k + 1, slab)), (lambda: rows_of(dw, z + k - 1, slab))
+        return net.step(k, up, down, up, down).start()
+
+    for k in range(3, top):
+        d_line.wait_recv()
+        d_line = d_step(k)
+        if k + 1 < top:
+            gu_line.wait_recv()
+            gu_line = gu_step(k + 1)
+    gather.forward()
+    gather.across()
+    gather.finish()
+    gu_line.wait_recv()
+    d_line.wait_recv()
+    for copy in crossing:
+        copy.wait_recv()
+    for made in kept:
+        made.wait()
+    net.finish()
+
+
+class LineSum:
+    def scratch(top, slab, width):
+        return [pltpu.VMEM((2, top, slab, width), BF), pltpu.VMEM((2, slab, width), BF)]
+
+    def __init__(self, net, grads, slab, land, term):
+        self.net, self.grads, self.land, self.term, self.slab = net, grads, land, term, slab
+        z, top = net.z, net.top
+        self.before = (z > 0, z < top - 1)
+        self.after = (z < top - 1, z > 0)
+
+    def block(self, i):
+        return rows_of(self.grads, i, self.slab)
+
+    def fetch(self, k):
+        z, top, net = self.net.z, self.net.top, self.net
+        self.has = ((z <= k - 1) & self.after[0], (z >= top - k) & self.after[1])
+        self.got = []
+        for d, i in ((0, z + top - k), (1, z - top + k)):
+            src = functools.partial(self.block, i)
+            land = lambda d=d: self.land.at[d, k - 1]
+            term = lambda d=d: self.term.at[d]
+            self.got.append(net.put(src, term, self.has[d] & self.before[d]))
+            self.got.append(net.put(src, land, self.has[d] & jnp.logical_not(self.before[d])))
+
+    def send(self, k):
+        net, z, top = self.net, self.net.z, self.net.top
+        for got in self.got:
+            got.wait()
+        if k > 1:
+            self.arriving.wait_recv()
+        for d in (0, 1):
+
+            @pl.when(self.has[d] & self.before[d])
+            def _(d=d):
+                land, term = self.land.at[d, k - 1], self.term.at[d]
+
+                def body(r):
+                    land[r] = (land[r].astype(F32) + term[r].astype(F32)).astype(BF)
+
+                for_rows(self.slab, body)
+
+        arrives = (self.before[0] & (z <= k), self.before[1] & (z >= top - 1 - k))
+        items = []
+        for d, to in ((0, net.up), (1, net.down)):
+            src = lambda d=d: self.land.at[d, k - 1]
+            dst = lambda d=d: self.land.at[d, k]
+            items += net.remote(src, dst, to, self.has[d], arrives[d]).items
+        self.arriving = Copies(items).start()
+
+    def fetch_own(self):
+        self.own = self.net.put(lambda: self.block(self.net.z), lambda: self.term.at[0])
+
+    def total(self, out):
+        self.own.wait()
+        self.arriving.wait_recv()
+        last = self.net.top - 1
+        term, up, down = self.term.at[0], self.land.at[0, last], self.land.at[1, last]
+
+        def run(*refs):
+            def body(r):
+                out[r] = sum(ref[r].astype(F32) for ref in refs).astype(BF)
+
+            for_rows(self.slab, body)
+
+        below, above = self.before
+        pl.when(below & above)(lambda: run(term, up, down))
+        pl.when(below & jnp.logical_not(above))(lambda: run(term, up))
+        pl.when(above & jnp.logical_not(below))(lambda: run(term, down))
+
+
+def back_kernel(
+    n, p1, p0, resid_ref, cot_ref, gain_ref, gu_grad,
+    out, grad_resid_ref, gu_sum, own, rc, rx, ry, r2, mine, land, term, sends, recvs, locals_,
+):
+    net = Net(n, sends, recvs, locals_)
+    top = net.top
+    slab = gu_sum.shape[0]
+    net.barrier((net.X, net.Y, net.C), line=True)
+    line = LineSum(net, gu_grad, slab, land, term)
+    red = Reduce(net, p1, p0, own, rc, rx, ry, r2)
+    line.fetch(1)
+    red.send_core()
+    line.send(1)
+    red.first()
+    line.fetch(2)
+    red.second()
+    line.send(2)
+    half, cut = rc.shape[1], red.cut
+
+    def norm_back(at, total):
+        resid = resid_ref[at]
+        inv = lax.rsqrt(jnp.mean(resid * resid, axis=-1, keepdims=True) + 1e-05)
+        grad = cot_ref[at].astype(F32) + rms_back(total, resid * inv, inv, gain_ref[...])
+        grad_resid_ref[at] = grad
+        mine[at] = grad.astype(BF)
+
+    gather = Gather(net, out, half)
+    part = lambda hf: functools.partial(rows_of, mine, hf, cut)
+    for hf in (0, 1):
+        red.last(hf, norm_back)
+        gather.send(hf, part(hf))
+    gather.send_rest([part(0), part(1)])
+    kept = net.put(lambda: mine, lambda: out.at[0])
+    line.fetch(3)
+    gather.forward()
+    gather.across()
+    line.send(3)
+    gather.finish()
+    for k in range(4, top):
+        line.fetch(k)
+        line.send(k)
+    line.fetch_own()
+    line.total(gu_sum)
+    kept.wait()
+    net.finish()
+
+
+def final_kernel(
+    n, p1, p0, at_grad, gu_sum, d_sum,
+    sum_ref, gu_out, d_out, at_out, own, rc, rx, ry, r2, mine, land, term, at_sum, sends, recvs, locals_,
+):
+    net = Net(n, sends, recvs, locals_)
+    top, c = net.top, net.c
+    slab = at_sum.shape[0]
+    db = slab // PLANE
+    net.barrier((net.X, net.Y, net.D, net.C), line=True)
+    line = LineSum(net, at_grad, slab, land, term)
+    red = Reduce(net, p1, p0, own, rc, rx, ry, r2)
+    line.fetch(1)
+    red.send_core()
+    line.send(1)
+    red.first()
+    line.fetch(2)
+    red.second()
+    line.send(2)
+    gu_parts = PartsBack(net, gu_sum, gu_out, db)
+    d_parts = PartsBack(net, d_sum, d_out, db)
+    half, cut = rc.shape[1], red.cut
+    line.fetch(3)
+
+    def keep(at, total):
+        mine[at] = total.astype(BF)
+
+    across = []
+    for hf in (0, 1):
+        red.last(hf, keep)
+        part = functools.partial(rows_of, mine, hf, cut)
+        across.append(net.remote(part, lambda hf=hf: sum_ref.at[c, pl.ds(hf * cut, cut)], net.C).start())
+    kept = net.put(lambda: mine, lambda: sum_ref.at[c])
+    line.send(3)
+    for k in range(4, top):
+        line.fetch(k)
+        line.send(k)
+    line.fetch_own()
+    line.total(at_sum)
+    at_parts = PartsBack(net, at_sum, at_out, db)
+    for parts in (gu_parts, d_parts, at_parts):
+        parts.wait()
+    for copy in across:
+        copy.wait_recv()
+    kept.wait()
+    net.finish()
+
+
+class PartsBack:
+    def __init__(self, net, src, out, rows):
+        self.own = net.put(lambda: rows_of(src, net.p, rows), lambda: out.at[net.p])
+        self.sent = [
+            net.remote(functools.partial(lambda j: rows_of(src, net.part[j], rows), j), lambda: out.at[net.p], to).start()
+            for j, to in ((1, net.X), (2, net.Y), (3, net.D))
+        ]
+
+    def wait(self):
+        self.own.wait()
+        for copy in self.sent:
+            copy.wait_recv()
+
+
 def cost(flops, nbytes):
     return pl.CostEstimate(flops=int(flops), bytes_accessed=int(nbytes), transcendentals=0)
 
@@ -402,6 +1010,25 @@
     def slot_first_other(g):
         return (g % PLANE) * 2 + 1 - g // PLANE
 
+    top = me.groups
+    slab = PLANE * db
+    cut = half_rows // 2
+    anywhere, in_vmem = pl.BlockSpec(memory_space=pl.ANY), pl.BlockSpec(memory_space=pltpu.VMEM)
+    sems = [pltpu.SemaphoreType.DMA((N_SEMS,))] * 3
+    shape = lambda *dims: jax.ShapeDtypeStruct(dims, BF)
+
+    def net_call(kernel, name, cid, args, in_specs, outs, out_specs, scratch):
+        return pl.pallas_call(
+            functools.partial(kernel, me.n),
+            in_specs=in_specs,
+            out_specs=out_specs,
+            out_shape=outs,
+            scratch_shapes=[*scratch, *sems],
+            compiler_params=pltpu.CompilerParams(collective_id=cid, has_side_effects=True, vmem_limit_bytes=VMEM),
+            cost_estimate=cost(10**8, 10**8),
+            name=name,
+        )(*args)
+
     def by_part(w, parts=PLANE):
         return w.reshape(w.shape[0], parts, w.shape[1] // parts).transpose(1, 0, 2)
 
@@ -414,25 +1041,42 @@
     g_main, g_rest = split_hidden(w_gate)
     u_main, u_rest = split_hidden(w_up)
     gu_pack = jnp.concatenate([g_main, u_main, g_rest, u_rest], axis=2)
-    down_pack = jnp.concatenate(
-        [w_down[: PLANE * main].reshape(PLANE, main, db), w_down[PLANE * main :].reshape(PLANE, rest, db)], axis=1
+    d_main, d_rest = split_hidden(w_down.T)
+    down_pack = jnp.concatenate([d_main, d_rest, jnp.zeros((PLANE, db, 64), BF)], axis=2)
+    wide = 2 * main + 2 * rest
+    tall = main + 128
+
+    def my_half(v):
+        return lax.dynamic_slice_in_dim(v, me.c * half_rows, half_rows, 0)
+
+    x_all, attn_w, gu0, gu_up1, gu_down1, d0 = net_call(
+        start_kernel,
+        "start",
+        1,
+        (layer_input, attn_pack, gu_pack, down_pack),
+        [in_vmem] * 4,
+        [
+            shape(slots, half_rows, width),
+            shape(width, 5 * DV),
+            shape(slab, wide),
+            shape(slab, wide),
+            shape(slab, wide),
+            shape(slab, tall),
+        ],
+        [anywhere] * 6,
+        [],
     )
-    attn_w = jnp.concatenate(me.gather_line(jnp.concatenate(me.spread(attn_pack), axis=0)), axis=0)
-    gu_w = jnp.concatenate(me.gather_line(jnp.concatenate(me.spread(gu_pack), axis=0)), axis=0)
-    down_w = jnp.concatenate(me.gather_line(jnp.concatenate(me.spread(down_pack), axis=1)), axis=1)
-    down_w = jnp.concatenate([down_w, jnp.zeros((64, width), BF)], axis=0)
+    gu_up2 = me.along(gu_up1, 1, range(1, top))
+    gu_down2 = me.along(gu_down1, -1, range(0, top - 1))
+    d_up1 = me.along(d0, 1, range(top))
+    d_down1 = me.along(d0, -1, range(top))
+    cot_mine = my_half(cotangent)
+    cot_x, cot_y = me.flip(cot_mine, 1), me.flip(cot_mine, 2)
+    cot_a, cot_b = me.flip(cot_y[:cut], 1), me.flip(cot_x[cut:], 2)
+
     w_qkv, w_o = attn_w[:, : 3 * DV], attn_w[:, 3 * DV :]
     gain_one = attn_w[:, 2 * DV + 64].astype(F32)[None, :]
     gain_two = attn_w[:, 2 * DV + 65].astype(F32)[None, :]
-
-    def my_half(v):
-        return lax.dynamic_slice_in_dim(v, me.c * half_rows, half_rows, 0)
-
-    def other_half(v):
-        return lax.dynamic_slice_in_dim(v, (1 - me.c) * half_rows, half_rows, 0)
-
-    x_all = me.gather8(my_half(layer_input), other_half(layer_input))
-    cot_all = me.gather8(my_half(cotangent), other_half(cotangent))
 
     params = pltpu.CompilerParams(dimension_semantics=("arbitrary",), vmem_limit_bytes=VMEM)
     row_block = lambda cols: pl.BlockSpec((1, half_rows, cols), lambda g: (g, 0, 0))
@@ -478,7 +1122,6 @@
     def start_at(pos):
         return jnp.max(jnp.where(starts <= pos, starts, 0))
 
-    top = me.groups
     reach = start_at(first - 1)
     enter = jnp.zeros((2, FE, 2 * DV), F32)
     for hop in range(1, top):
@@ -522,48 +1165,65 @@
         name="attend",
     )(sc, qkv, before, enter, maps, w_o)
 
-    x_mine = my_half(layer_input).astype(F32)
-    resid = x_mine + me.reduce8(attn_other, attn_own)
-    inv_two = rms_parts(resid)
-    x_hat_two = resid * inv_two
-    normed_mlp = me.gather8((x_hat_two * gain_two).astype(BF))
-
-    wide = 2 * main + 2 * rest
-    tall = main + 128
-    hid, grad_gu, gn_other, gn_own = pl.pallas_call(
-        mlp_kernel,
+    reduce_scratch = Reduce.scratch(PLANE, half_rows, width)
+    mine_scratch = pltpu.VMEM((half_rows, width), BF)
+    rows_f32 = jax.ShapeDtypeStruct((half_rows, width), F32)
+    normed_mlp, resid, gu_far, d_far, cot_all = net_call(
+        norm_kernel,
+        "norm",
+        2,
+        (
+            attn_other, attn_own, my_half(layer_input), gain_two, gu_up2, gu_down2, d_up1, d_down1,
+            cotangent, cot_x, cot_y, cot_a, cot_b,
+        ),
+        [anywhere, anywhere, in_vmem, in_vmem, *[anywhere] * 4, *[in_vmem] * 5],
+        [shape(slots, half_rows, width), rows_f32, shape(width, wide), shape(width, tall), shape(slots, half_rows, width)],
+        [anywhere, in_vmem, anywhere, anywhere, anywhere],
+        [*reduce_scratch, mine_scratch],
+    )
+
+    hid, grad_gu, gn_other, gn_own, down_w = pl.pallas_call(
+        functools.partial(mlp_kernel, top),
         grid=(slots,),
         in_specs=[
             pl.BlockSpec((1, half_rows, width), lambda g: (slot_first_other(g), 0, 0)),
             pl.BlockSpec((1, half_rows, width), lambda g: (slot_first_other(g), 0, 0)),
-            whole(width, wide),
-            whole(tall, width),
+            *[anywhere] * 10,
         ],
         out_specs=[
             pl.BlockSpec((1, half_rows, tall), lambda g: (slot_first_other(g), 0, 0)),
             pl.BlockSpec((1, half_rows, wide), lambda g: (slot_first_other(g), 0, 0)),
             *part_specs,
+            anywhere,
         ],
-        out_shape=[
-            jax.ShapeDtypeStruct((slots, half_rows, tall), BF),
-            jax.ShapeDtypeStruct((slots, half_rows, wide), BF),
-            *part_shapes,
+        out_shape=[shape(slots, half_rows, tall), shape(slots, half_rows, wide), *part_shapes, shape(width, tall)],
+        scratch_shapes=[
+            pltpu.VMEM((width, wide), BF),
+            pltpu.VMEM((width, tall), BF),
+            pltpu.SemaphoreType.DMA((4 * top,)),
+            pltpu.SemaphoreType.DMA((1,)),
         ],
         compiler_params=params,
         cost_estimate=cost(2 * group_rows * width * (2 * wide + tall), 2**25),
         name="mlp",
-    )(normed_mlp, cot_all, gu_w, down_w)
-
-    grad_normed_mlp = me.reduce8(gn_other, gn_own)
-    grad_resid = my_half(cotangent).astype(F32) + rms_back(grad_normed_mlp, x_hat_two, inv_two, gain_two)
-    grad_attn = me.gather8(grad_resid.astype(BF))
+    )(normed_mlp, cot_all, gu0, gu_up1, gu_down1, gu_up2, gu_down2, gu_far, d0, d_up1, d_down1, d_far)
 
     def flat(v):
         return v.reshape(slots * half_rows, v.shape[2])
 
     gu_grad = dot(flat(normed_mlp), flat(grad_gu), TN).astype(BF)
-    down_grad = dot(flat(hid), flat(cot_all), TN).astype(BF)
-    lo = dot(flat(hid), down_w).astype(BF).reshape(PLANE, 2, half_rows, width)
+    grad_attn, grad_resid, gu_sum = net_call(
+        back_kernel,
+        "back",
+        3,
+        (gn_other, gn_own, resid, cot_mine, gain_two, gu_grad),
+        [anywhere, anywhere, in_vmem, in_vmem, in_vmem, anywhere],
+        [shape(slots, half_rows, width), rows_f32, shape(slab, wide)],
+        [anywhere, in_vmem, in_vmem],
+        [*reduce_scratch, mine_scratch, *LineSum.scratch(top, slab, wide)],
+    )
+    down_grad = dot(flat(cot_all), flat(hid), TN).astype(BF)
+    lo = dot(flat(hid), down_w, NT).astype(BF).reshape(PLANE, 2, half_rows, width)
     mlp_sum = me.reduce8(lo[:, 1], lo[:, 0])
     layer_out = me.both((resid + mlp_sum).astype(BF))
 
@@ -620,39 +1280,41 @@
         name="grads",
     )(sc, qkv, gaug, before, enter, after, leave, maps, w_qkv)
 
-    grad_normed = me.reduce8(ga_other, ga_own).astype(BF)
-    grad_normed_both = me.both(grad_normed).astype(F32)
+    qkv_grad = dot(flat(normed), flat(dqkv), TN).astype(BF)
+    o_grad = dot(flat(grad_attn), flat(mixed), TN).astype(BF)
+    attn_grad = jnp.concatenate([qkv_grad, o_grad], axis=1)
+
+    def row_piece(v):
+        return lambda i: lax.dynamic_slice_in_dim(v, i * slab, slab, 0)
+
+    d_sum = me.scatter_line(row_piece(down_grad)).astype(BF)
+    grad_normed_both, gu_parts, down_parts, attn_parts = net_call(
+        final_kernel,
+        "final",
+        4,
+        (ga_other, ga_own, attn_grad, gu_sum, d_sum),
+        [anywhere, anywhere, anywhere, in_vmem, in_vmem],
+        [
+            shape(2, half_rows, width),
+            shape(PLANE, db, wide),
+            shape(PLANE, db, tall),
+            shape(PLANE, db, 5 * DV),
+        ],
+        [anywhere] * 4,
+        [*reduce_scratch, mine_scratch, *LineSum.scratch(top, slab, 5 * DV), pltpu.VMEM((slab, 5 * DV), BF)],
+    )
+    grad_normed_both = grad_normed_both.reshape(rows, width).astype(F32)
     grad_resid_both = me.both(grad_resid)
     x_float = layer_input.astype(F32)
     inv_one = rms_parts(x_float)
     input_grad = grad_resid_both + rms_back(grad_normed_both, x_float * inv_one, inv_one, gain_one)
 
-    qkv_grad = dot(flat(normed), flat(dqkv), TN).astype(BF)
-    o_grad = dot(flat(grad_attn), flat(mixed), TN).astype(BF)
-    attn_grad = jnp.concatenate([qkv_grad, o_grad], axis=1)
-    slab = PLANE * db
-
-    def row_piece(v):
-        return lambda i: lax.dynamic_slice_in_dim(v, i * slab, slab, 0)
-
-    def col_piece(v):
-        return lambda i: lax.dynamic_slice_in_dim(v, i * slab, slab, 1)
-
-    gu_sum = me.scatter_line(row_piece(gu_grad)).astype(BF)
-    down_sum = me.scatter_line(col_piece(down_grad[: main + rest])).astype(BF)
-    attn_sum = me.scatter_line(row_piece(attn_grad)).astype(BF)
-    gu_parts = me.spread(gu_sum.reshape(PLANE, db, wide))
-    down_parts = me.spread(down_sum.reshape(main + rest, PLANE, db).transpose(1, 0, 2))
-    attn_parts = me.spread(attn_sum.reshape(PLANE, db, 5 * DV))
-
     def cols(parts, a, b):
-        return [v[:, a:b].astype(F32) for v in parts]
+        return [parts[q, :, a:b].astype(F32) for q in range(PLANE)]
 
     gate_grad = jnp.concatenate(cols(gu_parts, 0, main) + cols(gu_parts, 2 * main, 2 * main + rest), axis=1)
     up_grad = jnp.concatenate(cols(gu_parts, main, 2 * main) + cols(gu_parts, 2 * main + rest, wide), axis=1)
-    down_out = jnp.concatenate(
-        [v[:main].astype(F32) for v in down_parts] + [v[main:].astype(F32) for v in down_parts], axis=0
-    )
+    down_out = jnp.concatenate(cols(down_parts, 0, main) + cols(down_parts, main, main + rest), axis=1).T
     value_grad = jnp.concatenate(cols(attn_parts, 0, 2 * DV), axis=1)
     query_grad = jnp.concatenate(cols(attn_parts, 2 * DV, 2 * DV + 2 * FD), axis=1)
     key_grad = jnp.concatenate(cols(attn_parts, 2 * DV + 2 * FD, 2 * DV + 4 * FD), axis=1)

time: 996 us -> 835 us (0.84)
  Pallas kernels: 118 us -> 523 us
  waiting for transfers between devices: 344 us -> 73.8 us
  starting transfers between devices: 208 us -> 68.7 us
  other arithmetic: 153 us -> 47.8 us
  local copies, waits for them, and re-layouts: 107 us -> 51.7 us
    pallas_call x1 -> x5, Pallas kernels: 47.4 us -> 453 us  [the longest x4 405 us: net_call(): pl.pallas_call(functools.partial(kernel, me.n), in_specs=in_specs, out_sp...]
    ppermute x52 -> x10, waiting for transfers between devices: 169 us -> 31.9 us  [flip(): return lax.ppermute(v, 'seq', [(s, s ^ bits) for s in range(self.n)])]
    ppermute x48 -> x22, waiting for transfers between devices: 173 us -> 40.8 us  [along(): return lax.ppermute(v, 'seq', pairs)]
    ppermute x48 -> x22, starting transfers between devices: 148 us -> 56.9 us  [along(): return lax.ppermute(v, 'seq', pairs)]
    ppermute x52 -> x10, starting transfers between devices: 56.5 us -> 11.2 us  [flip(): return lax.ppermute(v, 'seq', [(s, s ^ bits) for s in range(self.n)])]
    unnamed x215 -> x125, local copies, waits for them, and re-layouts: 51.3 us -> 17.7 us
    concatenate x8 -> x1, other arithmetic: 28.5 us -> 1.05 us  [shards(): jnp.concatenate([d_main, d_rest, jnp.zeros((PLANE, db, 64), BF)], axis=2)]
    add x4 -> x1, other arithmetic: 32.1 us -> 8.96 us  [reduce8(): total = own_half.astype(F32) + self.core(other_half).astype(F32)]
  transfers between devices with their start and end apart: 127 -> 37, of which waited for: 45 -> 14; matrix products, arithmetic and copies ran while one was open for 28% -> 9% of each run, Pallas kernels for 12% -> 14%
where the time goes in v2:
time: 835 us; the launch traced here: 825 us
  Pallas kernels  523 us (63%)
  waiting for transfers between devices  73.8 us (9%)
  starting transfers between devices  68.7 us (8%)
  local copies, waits for them, and re-layouts  51.7 us (6%)
  matrix products  51.7 us (6%)
  other arithmetic  47.8 us (6%)
    pallas_call x4, Pallas kernels, net_call(): pl.pallas_call(functools.partial(kernel, me.n), in_specs=in_specs, out_sp...  405 us
    ppermute x22, starting transfers between devices, along(): return lax.ppermute(v, 'seq', pairs)  56.9 us
    dot_general x5, matrix products, dot(): return lax.dot_general(a, b, dims, preferred_element_type=F32)  51.7 us
    pallas_call x1, Pallas kernels, shards(): pl.pallas_call(functools.partial(mlp_kernel, top), grid=(slots,), in_spec...  48.5 us
    ppermute x22, waiting for transfers between devices, along(): return lax.ppermute(v, 'seq', pairs)  40.8 us
    ppermute x10, waiting for transfers between devices, flip(): return lax.ppermute(v, 'seq', [(s, s ^ bits) for s in range(self.n)])  31.9 us
    pallas_call x1, Pallas kernels, shards(): pl.pallas_call(functools.partial(grads_kernel, n_seq, slot_first_other),...  25.8 us
    unnamed x125, local copies, waits for them, and re-layouts  17.7 us
  transfers between devices with their start and end apart: 37, of which 14 were waited for; matrix products, arithmetic and copies ran while one was open for 9% of the time, Pallas kernels for 14%

profile of v2, /device:TPU:0, one launch (start us, length us, event | category | flops | bytes accessed | tf_op | source)
XLA Modules:
  0.0 825.1 jit_solution(2827909778918274895)
XLA Ops:
  13.5 3.1 concatenate.68.gp
  17.9 106.1 %start.1 = (bf16[8,256,2048]{2,1,0:T(8,128)(2,1)}, bf16[2048,640]{1,0:T(8,128)(2,1)}, bf16[512,1408]{1,0:T(8,128)(2,1)S(1)}, bf16[512,1408]{1,0:T(8,128)(2,1)S(1...) custom-call(bf16[512,2048]{1,0:T(8,128)(2,1)} %x.1, bf16[4,128,640]{2,1,0:T(8,128)(2,1)S(1)} %concatenate.67.ap, ...), custom_call_target="tpu_custom_call" | custom-call | flops 100000000 | bytes 100000000 | tf_op jit(solution)/shard_map/start/pallas_call | solution.py:1021
  127.1 2.0 convert_reduce_fusion
  131.0 11.1 %project.1 = (bf16[8,256,2048]{2,1,0:T(8,128)(2,1)}, bf16[8,256,384]{2,1,0:T(8,128)(2,1)S(1)}) custom-call(bf16[8,256,2048]{2,1,0:T(8,128)(2,1)} %get-tuple-element.49.x_ref, f32[1,2048]{1,0:T(1,128)S(1)} %bitcast.176, bf16[2048,384]{1,0:T(8,128)(2,1)S(1)} %slice.226.w_ref), custom_call_target="tpu_custom_call" | custom-call | flops 3221225472 | bytes 16777216 | tf_op jit(solution)/shard_map/project/pallas_call | solution.py:1085
  142.1 6.2 states.1
  149.4 4.3 collective-permute-start.2
  153.7 2.0 collective-permute-start.1
  155.7 3.1 collective-permute-start
  168.7 14.9 %attend.1 = (bf16[4,256,2048]{2,1,0:T(8,128)(2,1)}, bf16[4,256,2048]{2,1,0:T(8,128)(2,1)}, bf16[8,256,256]{2,1,0:T(8,128)(2,1)S(1)}, f32[8,256,128]{2,1,0:T(8,128)S(1)}) custom-call(s32[6]{0:T(128)S(1)} %pad_add_fusion.sc, bf16[8,256,384]{2,1,0:T(8,128)(2,1)} %copy-done.19, bf16[8,2,160,256]{3,2,1,0:T(8,128)(2,1)S(1)} %copy-done.21, ...), custom_call_target="tpu_custom_call" | custom-call | flops 6400000000 | bytes 16777216 | tf_op jit(solution)/shard_map/attend/pallas_call | solution.py:1144
  193.4 2.2 collective-permute-done.30
  195.6 6.9 collective-permute-start.35
  203.8 5.4 collective-permute-start.33
  209.3 4.0 collective-permute-done.34
  215.8 2.9 collective-permute-done.32
  218.7 1.8 collective-permute-start.3
  224.4 5.5 collective-permute-start.5
  229.9 3.5 collective-permute-start.31
  234.8 1.9 slice.292
  236.7 7.2 collective-permute-done.31
  251.5 4.0 collective-permute-done.4.gd2
  257.1 110.8 %norm.1 = (bf16[8,256,2048]{2,1,0:T(8,128)(2,1)}, f32[256,2048]{1,0:T(8,128)}, bf16[2048,1408]{1,0:T(8,128)(2,1)}, bf16[2048,768]{1,0:T(8,128)(2,1)}, bf16[8,256,2048]{2,1,0:T(8,128)(2,1)}) custom-call(bf16[4,256,2048]{2,1,0:T(8,128)(2,1)} %get-tuple-element.54.p1, bf16[4,256,2048]{2,1,0:T(8,128)(2,1)} %get-tuple-element.55.p0, ...), custom_call_target="tpu_custom_call" | custom-call | flops 100000000 | bytes 100000000 | tf_op jit(solution)/shard_map/norm/pallas_call | solution.py:1021
  368.0 48.5 %mlp.1 = (bf16[8,256,768]{2,1,0:T(8,128)(2,1)}, bf16[8,256,1408]{2,1,0:T(8,128)(2,1)}, bf16[4,256,2048]{2,1,0:T(8,128)(2,1)}, bf16[4,256,2048]{2,1,0:T(8,128)(2,1)}, bf16[2048,768]{1,0:T(8,128)(2,1)}) custom-call(bf16[8,256,2048]{2,1,0:T(8,128)(2,1)} %get-tuple-element.60.n_ref, bf16[8,256,2048]{2,1,0:T(8,128)(2,1)} %get-tuple-element.61.cot_ref, ...), custom_call_target="tpu_custom_call" | custom-call | flops 30064771072 | bytes 33554432 | tf_op jit(solution)/shard_map/mlp/pallas_call | solution.py:1185
  416.5 19.2 %bitcast_convert_fusion.gu_grad = bf16[2048,1408]{1,0:T(8,128)(2,1)} fusion(bf16[8,256,2048]{2,1,0:T(8,128)(2,1)} %get-tuple-element.60.n_ref, bf16[8,256,1408]{2,1,0:T(8,128)(2,1)} %get-tuple-element.69), kind=kOutput, calls=%fused_computation | convolution fusion | flops 11814043648 | bytes 19922944 | tf_op jit(solution)/shard_map/dot_general | solution.py:26
  435.7 111.6 %back.1 = (bf16[8,256,2048]{2,1,0:T(8,128)(2,1)}, f32[256,2048]{1,0:T(8,128)S(1)}, bf16[512,1408]{1,0:T(8,128)(2,1)S(1)}) custom-call(bf16[4,256,2048]{2,1,0:T(8,128)(2,1)} %get-tuple-element.67.p1, bf16[4,256,2048]{2,1,0:T(8,128)(2,1)} %get-tuple-element.68.p0, f32[256,2048]{1,0:T(8,128)} %get-tuple-element.59.resid_ref, ...), custom_call_target="tpu_custom_call" | custom-call | flops 100000000 | bytes 100000000 | tf_op jit(solution)/shard_map/back/pallas_call | solution.py:1021
  547.4 6.0 fusion.7
  553.5 12.3 %grads_in.1 = (bf16[8,256,512]{2,1,0:T(8,128)(2,1)}, bf16[8,2,160,256]{3,2,1,0:T(8,128)(2,1)S(1)}, bf16[2,160,256]{2,1,0:T(8,128)(2,1)S(1)}) custom-call(s32[6]{0:T(128)S(1)} %pad_add_fusion.sc, bf16[8,256,2048]{2,1,0:T(8,128)(2,1)} %get-tuple-element.71.ga_ref, bf16[2048,256]{1,0:T(8,128)(2,1)S(1)} %copy-done.4, bf16[8,256,384]{2,1,0:T(8,128)(2,1)} %copy-done.19, ...), custom_call_target="tpu_custom_call" | custom-call | flops 6400000000 | bytes 16777216 | tf_op jit(solution)/shard_map/grads_in/pallas_call | solution.py:1233
  569.6 9.4 %bitcast_convert_fusion.1 = bf16[2048,768]{1,0:T(8,128)(2,1)S(1)} fusion(bf16[8,256,2048]{2,1,0:T(8,128)(2,1)} %get-tuple-element.61.cot_ref, bf16[8,256,768]{2,1,0:T(8,128)(2,1)S(1)} %copy-done.56), kind=kOutput, calls=%fused_computation.3 | convolution fusion | flops 6444023808 | bytes 14680064 | tf_op jit(solution)/shard_map/dot_general | solution.py:26
  580.0 4.7 collective-permute-start.21
  585.4 9.1 %convolution_convert_fusion = bf16[2048,2048]{1,0:T(8,128)(2,1)S(1)} fusion(bf16[2048,768]{1,0:T(8,128)(2,1)S(1)} %bitcast.205, bf16[2048,768]{1,0:T(8,128)(2,1)} %get-tuple-element.66), kind=kOutput, calls=%fused_computation.2 | convolution fusion | flops 6446645248 | bytes 14680064 | tf_op jit(solution)/shard_map/dot_general | solution.py:26
  594.6 2.3 slice_bitcast_fusion
  596.9 2.2 copy-done.28
  600.8 4.9 collective-permute-start.22
  605.7 25.8 %grads.1 = (bf16[4,256,2048]{2,1,0:T(8,128)(2,1)}, bf16[4,256,2048]{2,1,0:T(8,128)(2,1)}, bf16[8,256,384]{2,1,0:T(8,128)(2,1)S(1)}) custom-call(s32[6]{0:T(128)S(1)} %pad_add_fusion.sc, bf16[8,256,384]{2,1,0:T(8,128)(2,1)} %copy-done.19, bf16[8,256,512]{2,1,0:T(8,128)(2,1)} %get-tuple-element.74.gaug_ref, bf16[8,2,160,256]{3,2,1,0:T(8,128)(2,1)S(1)} %copy-done.22, ...), custom_call_target="tpu_custom_call" | custom-call | flops 12800000000 | bytes 16777216 | tf_op jit(solution)/shard_map/grads/pallas_call | solution.py:1260
  634.0 7.9 bitcast_convert_fusion.2
  645.1 1.7 pad_maximum_fusion.at_grad
  646.8 2.6 broadcast_select_fusion.1
  649.4 10.3 %collective-permute-done.23 = bf16[512,768]{1,0:T(8,128)(2,1)S(1)} collective-permute-done((bf16[512,768]{1,0:T(8,128)(2,1)S(1)}, bf16[512,768]{1,0:T(8,128)(2,1)S(1)}, u32[]{:S(2)}, u32[]{:S(2)}) %collective-permute-start.23) | collective-permute-done | bytes 786464 | tf_op jit(solution)/shard_map/ppermute | solution.py:329
  659.7 11.1 %collective-permute-done.26 = bf16[512,768]{1,0:T(8,128)(2,1)S(1)} collective-permute-done((bf16[512,768]{1,0:T(8,128)(2,1)S(1)}, bf16[512,768]{1,0:T(8,128)(2,1)S(1)}, u32[]{:S(2)}, u32[]{:S(2)}) %collective-permute-start.26) | collective-permute-done | bytes 786464 | tf_op jit(solution)/shard_map/ppermute | solution.py:329
  671.0 76.1 %final.1 = (bf16[2,256,2048]{2,1,0:T(8,128)(2,1)}, bf16[4,128,1408]{2,1,0:T(8,128)(2,1)S(1)}, bf16[4,128,768]{2,1,0:T(8,128)(2,1)S(1)}, bf16[4,128,640]{2,1,0:T(8,128)(2,1)S(1)}) custom-call(bf16[4,256,2048]{2,1,0:T(8,128)(2,1)} %get-tuple-element.77.p1, bf16[4,256,2048]{2,1,0:T(8,128)(2,1)} %get-tuple-element.78.p0, ...), custom_call_target="tpu_custom_call" | custom-call | flops 100000000 | bytes 100000000 | tf_op jit(solution)/shard_map/final/pallas_call | solution.py:1021
  756.4 9.0 %convert_add_fusion = (f32[4,256,2048]{2,1,0:T(8,128)}, bf16[4,256,2048]{2,1,0:T(8,128)(2,1)S(1)}) fusion(bf16[4,256,2048]{2,1,0:T(8,128)(2,1)} %collective-permute-done.11, bf16[4,2,256,2048]{3,2,1,0:T(8,128)(2,1)} %bitcast.180), kind=kLoop, calls=%fused_computation.1 | loop fusion | flops 8388608 | bytes 20971520 | tf_op jit(solution)/shard_map/add | solution.py:371
  770.8 1.9 concatenate.85
  772.7 2.5 fusion.2
  775.2 17.7 %collective-permute-done.12 = bf16[2,128,2048]{2,1,0:T(8,128)(2,1)} collective-permute-done((bf16[2,128,2048]{2,1,0:T(8,128)(2,1)}, bf16[2,128,2048]{2,1,0:T(8,128)(2,1)}, u32[]{:S(2)}, u32[]{:S(2)}) %collective-permute-start.12) | collective-permute-done | bytes 1048608 | tf_op jit(solution)/shard_map/ppermute | solution.py:318
  794.6 1.9 fusion.15
  796.9 1.7 collective-permute-start.15
  798.7 10.7 %collective-permute-done.13 = bf16[128,2048]{1,0:T(8,128)(2,1)S(1)} collective-permute-done((bf16[128,2048]{1,0:T(8,128)(2,1)S(1)}, bf16[128,2048]{1,0:T(8,128)(2,1)S(1)}, u32[]{:S(2)}, u32[]{:S(2)}) %collective-permute-start.13) | collective-permute-done | bytes 524320 | tf_op jit(solution)/shard_map/ppermute | solution.py:318
  809.5 2.2 fusion.14
  814.3 3.2 fusion.5
  (260 shorter events, 91.6 us)
Async XLA Ops:
  129.2 12.9 %copy-start.8 = (f32[2048]{0:T(1024)}, f32[2048]{0:T(1024)S(1)}, u32[]{:S(2)}) copy-start(f32[2048]{0:T(1024)S(1)} %get-tuple-element.123) | copy-start | bytes 24580
  142.1 16.7 %copy-start.32 = (bf16[512,2048]{1,0:T(8,128)(2,1)S(1)}, bf16[512,2048]{1,0:T(8,128)(2,1)}, u32[]{:S(2)}) copy-start(bf16[512,2048]{1,0:T(8,128)(2,1)} %cot.1) | copy-start | bytes 6291460
  149.4 15.7 %collective-permute-start.2 = (bf16[2,160,256]{2,1,0:T(8,128)(2,1)S(1)}, bf16[2,160,256]{2,1,0:T(8,128)(2,1)S(1)}, u32[]{:S(2)}, u32[]{:S(2)}) collective-permute-start(bf16[2,160,256]{2,1,0:T(8,128)(2,1)S(1)} %get-tuple-element.53), channel_id=1, source_target_pairs={{0,24},{2,26},{4,28},{6,30},{1,25},{3,27},{5,29},{7,31}} | collective-permute-start | bytes 491528 | tf_op jit(solution)/shard_map/ppermute | solution.py:329
  153.7 11.4 %collective-permute-start.1 = (bf16[2,160,256]{2,1,0:T(8,128)(2,1)S(1)}, bf16[2,160,256]{2,1,0:T(8,128)(2,1)}, u32[]{:S(2)}, u32[]{:S(2)}) collective-permute-start(bf16[2,160,256]{2,1,0:T(8,128)(2,1)S(1)} %get-tuple-element.53), channel_id=1, source_target_pairs={{0,16},{2,18},{4,20},{6,22},{8,24},{10,26},{12,28},{14,30},{1,17},... | collective-permute-start | bytes 491528 | tf_op jit(solution)/shard_map/ppermute | solution.py:329
  155.7 9.5 %collective-permute-start = (bf16[2,160,256]{2,1,0:T(8,128)(2,1)S(1)}, bf16[2,160,256]{2,1,0:T(8,128)(2,1)}, u32[]{:S(2)}, u32[]{:S(2)}) collective-permute-start(bf16[2,160,256]{2,1,0:T(8,128)(2,1)S(1)} %get-tuple-element.53), channel_id=1, source_target_pairs={{0,8},{2,10},{4,12},{6,14},{8,16},{10,18},{12,20},{14,22},{16,24},... | collective-permute-start | bytes 491528 | tf_op jit(solution)/shard_map/ppermute | solution.py:329
  158.9 65.6 %collective-permute-start.8 = (bf16[256,2048]{1,0:T(8,128)(2,1)S(1)}, bf16[256,2048]{1,0:T(8,128)(2,1)S(1)}, u32[]{:S(2)}, u32[]{:S(2)}) collective-permute-start(bf16[256,2048]{1,0:T(8,128)(2,1)S(1)} %constant_dynamic-slice_fusion.2.cot_ref), channel_id=1, source_target_pairs={{0,4},{2,6},{4,0},{6,2},{8,12},{10,14},{12,8},{14,10},{16,20},{18,... | collective-permute-start | bytes 3145736 | tf_op jit(solution)/shard_map/ppermute | solution.py:318
  160.5 69.5 %collective-permute-start.7 = (bf16[256,2048]{1,0:T(8,128)(2,1)S(1)}, bf16[256,2048]{1,0:T(8,128)(2,1)}, u32[]{:S(2)}, u32[]{:S(2)}) collective-permute-start(bf16[256,2048]{1,0:T(8,128)(2,1)S(1)} %constant_dynamic-slice_fusion.2.cot_ref), channel_id=1, source_target_pairs={{0,2},{2,0},{4,6},{6,4},{8,10},{10,8},{12,14},{14,12},{16,18},{18,... | collective-permute-start | bytes 3145736 | tf_op jit(solution)/shard_map/ppermute | solution.py:318
  162.3 21.3 %copy-start.3 = (bf16[2048,256]{1,0:T(8,128)(2,1)}, bf16[2048,256]{1,0:T(8,128)(2,1)S(1)}, u32[]{:S(2)}) copy-start(bf16[2048,256]{1,0:T(8,128)(2,1)S(1)} %slice.227.wo_ref) | copy-start | bytes 3145732
  186.2 47.3 %copy-start.25 = (bf16[512,2048]{1,0:T(8,128)(2,1)S(1)}, bf16[512,2048]{1,0:T(8,128)(2,1)}, u32[]{:S(2)}) copy-start(bf16[512,2048]{1,0:T(8,128)(2,1)} %x.1) | copy-start | bytes 6291460
  187.1 1.1 collective-permute-start.28
  188.3 3.6 collective-permute-start.29
  189.8 54.7 %collective-permute-start.6 = (bf16[512,768]{1,0:T(8,128)(2,1)}, bf16[512,768]{1,0:T(8,128)(2,1)S(1)}, u32[]{:S(2)}, u32[]{:S(2)}) collective-permute-start(bf16[512,768]{1,0:T(8,128)(2,1)} %copy-done.14), channel_id=1, source_target_pairs={{8,0},{10,2},{12,4},{14,6},{16,8},{18,10},{20,12},{22,14},{24,16},... | collective-permute-start | bytes 2359304 | tf_op jit(solution)/shard_map/ppermute | solution.py:329
  192.0 3.6 collective-permute-start.30
  195.6 8.2 collective-permute-start.35
  202.5 10.8 %collective-permute-start.34 = (f32[2,128]{1,0:T(2,128)S(1)}, f32[2,128]{1,0:T(2,128)S(1)}, u32[]{:S(2)}, u32[]{:S(2)}) collective-permute-start(f32[2,128]{1,0:T(2,128)S(1)} %max.54), channel_id=1, source_target_pairs={{16,0},{18,2},{20,4},{22,6},{24,8},{26,10},{28,12},{30,14},{17,1},... | collective-permute-start | bytes 3080 | tf_op jit(solution)/shard_map/ppermute | solution.py:329
  203.8 10.7 %collective-permute-start.33 = (f32[2,128]{1,0:T(2,128)S(1)}, f32[2,128]{1,0:T(2,128)S(1)}, u32[]{:S(2)}, u32[]{:S(2)}) collective-permute-start(f32[2,128]{1,0:T(2,128)S(1)} %max.54), channel_id=1, source_target_pairs={{0,16},{2,18},{4,20},{6,22},{8,24},{10,26},{12,28},{14,30},{1,17},... | collective-permute-start | bytes 3080 | tf_op jit(solution)/shard_map/ppermute | solution.py:329
  213.2 5.5 collective-permute-start.32
  214.5 7.3 collective-permute-start.36
  218.7 32.8 %collective-permute-start.3 = (bf16[512,1408]{1,0:T(8,128)(2,1)}, bf16[512,1408]{1,0:T(8,128)(2,1)}, u32[]{:S(2)}, u32[]{:S(2)}) collective-permute-start(bf16[512,1408]{1,0:T(8,128)(2,1)} %copy-done.12), channel_id=1, source_target_pairs={{8,16},{10,18},{12,20},{14,22},{16,24},{18,26},{20,28},{22,30},{9,... | collective-permute-start | bytes 4325384 | tf_op jit(solution)/shard_map/ppermute | solution.py:329
  221.8 33.6 %collective-permute-start.4 = (bf16[512,1408]{1,0:T(8,128)(2,1)}, bf16[512,1408]{1,0:T(8,128)(2,1)}, u32[]{:S(2)}, u32[]{:S(2)}) collective-permute-start(bf16[512,1408]{1,0:T(8,128)(2,1)} %get-tuple-element.57.gd1), channel_id=1, source_target_pairs={{8,0},{10,2},{12,4},{14,6},{16,8},{18,10},{20,12},{22,14},{9,1},{1... | collective-permute-start | bytes 4325384 | tf_op jit(solution)/shard_map/ppermute | solution.py:329
  224.4 27.0 %collective-permute-start.5 = (bf16[512,768]{1,0:T(8,128)(2,1)}, bf16[512,768]{1,0:T(8,128)(2,1)}, u32[]{:S(2)}, u32[]{:S(2)}) collective-permute-start(bf16[512,768]{1,0:T(8,128)(2,1)} %copy-done.14), channel_id=1, source_target_pairs={{0,8},{2,10},{4,12},{6,14},{8,16},{10,18},{12,20},{14,22},{16,24},... | collective-permute-start | bytes 2359304 | tf_op jit(solution)/shard_map/ppermute | solution.py:329
  229.9 14.0 %collective-permute-start.31 = (f32[2,128]{1,0:T(2,128)S(1)}, f32[2,128]{1,0:T(2,128)S(1)}, u32[]{:S(2)}, u32[]{:S(2)}) collective-permute-start(f32[2,128]{1,0:T(2,128)S(1)} %max.54), channel_id=1, source_target_pairs={{0,8},{2,10},{4,12},{6,14},{8,16},{10,18},{12,20},{14,22},{16,24},... | collective-permute-start | bytes 3080 | tf_op jit(solution)/shard_map/ppermute | solution.py:329
  243.9 11.5 %collective-permute-start.9 = (bf16[128,2048]{1,0:T(8,128)(2,1)}, bf16[128,2048]{1,0:T(8,128)(2,1)}, u32[]{:S(2)}, u32[]{:S(2)}) collective-permute-start(bf16[128,2048]{1,0:T(8,128)(2,1)} %slice.291), channel_id=1, source_target_pairs={{0,2},{2,0},{4,6},{6,4},{8,10},{10,8},{12,14},{14,12},{16,18},{18,... | collective-permute-start | bytes 1572872 | tf_op jit(solution)/shard_map/ppermute | solution.py:318
  245.4 10.6 %collective-permute-start.10 = (bf16[128,2048]{1,0:T(8,128)(2,1)}, bf16[128,2048]{1,0:T(8,128)(2,1)}, u32[]{:S(2)}, u32[]{:S(2)}) collective-permute-start(bf16[128,2048]{1,0:T(8,128)(2,1)} %slice.292), channel_id=1, source_target_pairs={{0,4},{2,6},{4,0},{6,2},{8,12},{10,14},{12,8},{14,10},{16,20},{18,... | collective-permute-start | bytes 1572872 | tf_op jit(solution)/shard_map/ppermute | solution.py:318
  257.1 110.8 %copy-start.7 = (bf16[512,768]{1,0:T(8,128)(2,1)S(1)}, bf16[512,768]{1,0:T(8,128)(2,1)}, u32[]{:S(2)}) copy-start(bf16[512,768]{1,0:T(8,128)(2,1)} %copy-done.5) | copy-start | bytes 2359300
  257.1 110.8 %copy-start.11 = (bf16[512,1408]{1,0:T(8,128)(2,1)S(1)}, bf16[512,1408]{1,0:T(8,128)(2,1)}, u32[]{:S(2)}) copy-start(bf16[512,1408]{1,0:T(8,128)(2,1)} %copy-done.10) | copy-start | bytes 4325380
  257.1 110.8 %copy-start.13 = (bf16[512,1408]{1,0:T(8,128)(2,1)S(1)}, bf16[512,1408]{1,0:T(8,128)(2,1)}, u32[]{:S(2)}) copy-start(bf16[512,1408]{1,0:T(8,128)(2,1)} %copy-done.12) | copy-start | bytes 4325380
  257.1 110.9 %copy-start.15 = (bf16[512,768]{1,0:T(8,128)(2,1)S(1)}, bf16[512,768]{1,0:T(8,128)(2,1)}, u32[]{:S(2)}) copy-start(bf16[512,768]{1,0:T(8,128)(2,1)} %copy-done.14) | copy-start | bytes 2359300
  435.7 111.6 %copy-start.24 = (bf16[8,256,256]{2,1,0:T(8,128)(2,1)S(1)}, bf16[8,256,256]{2,1,0:T(8,128)(2,1)}, u32[]{:S(2)}) copy-start(bf16[8,256,256]{2,1,0:T(8,128)(2,1)} %copy-done.23) | copy-start | bytes 3145732
  553.4 16.2 %copy-start.56 = (bf16[8,256,768]{2,1,0:T(8,128)(2,1)S(1)}, bf16[8,256,768]{2,1,0:T(8,128)(2,1)}, u32[]{:S(2)}) copy-start(bf16[8,256,768]{2,1,0:T(8,128)(2,1)} %get-tuple-element.65) | copy-start | bytes 9437188
  565.7 33.4 %collective-permute-start.20 = (bf16[2,160,256]{2,1,0:T(8,128)(2,1)S(1)}, bf16[2,160,256]{2,1,0:T(8,128)(2,1)S(1)}, u32[]{:S(2)}, u32[]{:S(2)}) collective-permute-start(bf16[2,160,256]{2,1,0:T(8,128)(2,1)S(1)} %get-tuple-element.76), channel_id=1, source_target_pairs={{24,0},{26,2},{28,4},{30,6},{25,1},{27,3},{29,5},{31,7}} | collective-permute-start | bytes 491528 | tf_op jit(solution)/shard_map/ppermute | solution.py:329
  567.0 32.1 %collective-permute-start.19 = (bf16[2,160,256]{2,1,0:T(8,128)(2,1)S(1)}, bf16[2,160,256]{2,1,0:T(8,128)(2,1)S(1)}, u32[]{:S(2)}, u32[]{:S(2)}) collective-permute-start(bf16[2,160,256]{2,1,0:T(8,128)(2,1)S(1)} %get-tuple-element.76), channel_id=1, source_target_pairs={{16,0},{18,2},{20,4},{22,6},{24,8},{26,10},{28,12},{30,14},{17,1},... | collective-permute-start | bytes 491528 | tf_op jit(solution)/shard_map/ppermute | solution.py:329
  568.3 31.3 %collective-permute-start.18 = (bf16[2,160,256]{2,1,0:T(8,128)(2,1)S(1)}, bf16[2,160,256]{2,1,0:T(8,128)(2,1)S(1)}, u32[]{:S(2)}, u32[]{:S(2)}) collective-permute-start(bf16[2,160,256]{2,1,0:T(8,128)(2,1)S(1)} %get-tuple-element.76), channel_id=1, source_target_pairs={{8,0},{10,2},{12,4},{14,6},{16,8},{18,10},{20,12},{22,14},{24,16},... | collective-permute-start | bytes 491528 | tf_op jit(solution)/shard_map/ppermute | solution.py:329
  580.0 19.7 %collective-permute-start.21 = (bf16[512,768]{1,0:T(8,128)(2,1)S(1)}, bf16[512,768]{1,0:T(8,128)(2,1)S(1)}, u32[]{:S(2)}, u32[]{:S(2)}) collective-permute-start(bf16[512,768]{1,0:T(8,128)(2,1)S(1)} %get-tuple-element.150), channel_id=1, source_target_pairs={{0,8},{2,10},{4,12},{6,14},{1,9},{3,11},{5,13},{7,15}} | collective-permute-start | bytes 2359304 | tf_op jit(solution)/shard_map/ppermute | solution.py:329
  584.7 46.8 %collective-permute-start.24 = (bf16[512,768]{1,0:T(8,128)(2,1)}, bf16[512,768]{1,0:T(8,128)(2,1)S(1)}, u32[]{:S(2)}, u32[]{:S(2)}) collective-permute-start(bf16[512,768]{1,0:T(8,128)(2,1)} %get-tuple-element.151), channel_id=1, source_target_pairs={{24,16},{26,18},{28,20},{30,22},{25,17},{27,19},{29,21},{31,23}} | collective-permute-start | bytes 2359304 | tf_op jit(solution)/shard_map/ppermute | solution.py:329
  599.1 157.2 %collective-permute-start.11 = (bf16[4,256,2048]{2,1,0:T(8,128)(2,1)}, bf16[4,256,2048]{2,1,0:T(8,128)(2,1)}, u32[]{:S(2)}, u32[]{:S(2)}) collective-permute-start(bf16[4,256,2048]{2,1,0:T(8,128)(2,1)} %slice_bitcast_fusion), channel_id=1, source_target_pairs={{0,1},{1,0},{2,3},{3,2},{4,5},{5,4},{6,7},{7,6},{8,9},{9,8},{10,11... | collective-permute-start | bytes 12582920 | tf_op jit(solution)/shard_map/ppermute | solution.py:321
  599.1 47.7 %collective-permute-start.17 = (f32[256,2048]{1,0:T(8,128)S(1)}, f32[256,2048]{1,0:T(8,128)S(1)}, u32[]{:S(2)}, u32[]{:S(2)}) collective-permute-start(f32[256,2048]{1,0:T(8,128)S(1)} %get-tuple-element.70), channel_id=1, source_target_pairs={{0,1},{1,0},{2,3},{3,2},{4,5},{5,4},{6,7},{7,6},{8,9},{9,8},{10,11... | collective-permute-start | bytes 6291464 | tf_op jit(solution)/shard_map/ppermute | solution.py:321
  600.8 30.7 %collective-permute-start.22 = (bf16[512,768]{1,0:T(8,128)(2,1)}, bf16[512,768]{1,0:T(8,128)(2,1)}, u32[]{:S(2)}, u32[]{:S(2)}) collective-permute-start(bf16[512,768]{1,0:T(8,128)(2,1)} %add_convert_fusion.4), channel_id=1, source_target_pairs={{0,8},{2,10},{4,12},{6,14},{8,16},{10,18},{12,20},{14,22},{1,9},{3... | collective-permute-start | bytes 2359304 | tf_op jit(solution)/shard_map/ppermute | solution.py:329
  633.1 10.6 %collective-permute-start.25 = (bf16[512,768]{1,0:T(8,128)(2,1)S(1)}, bf16[512,768]{1,0:T(8,128)(2,1)S(1)}, u32[]{:S(2)}, u32[]{:S(2)}) collective-permute-start(bf16[512,768]{1,0:T(8,128)(2,1)S(1)} %get-tuple-element.149), channel_id=1, source_target_pairs={{16,8},{18,10},{20,12},{22,14},{24,16},{26,18},{28,20},{30,22},{17... | collective-permute-start | bytes 2359304 | tf_op jit(solution)/shard_map/ppermute | solution.py:329
  641.9 17.7 %collective-permute-start.23 = (bf16[512,768]{1,0:T(8,128)(2,1)S(1)}, bf16[512,768]{1,0:T(8,128)(2,1)S(1)}, u32[]{:S(2)}, u32[]{:S(2)}) collective-permute-start(bf16[512,768]{1,0:T(8,128)(2,1)S(1)} %get-tuple-element.148), channel_id=1, source_target_pairs={{0,8},{2,10},{4,12},{6,14},{8,16},{10,18},{12,20},{14,22},{16,24},... | collective-permute-start | bytes 2359304 | tf_op jit(solution)/shard_map/ppermute | solution.py:329
  643.8 26.9 %collective-permute-start.26 = (bf16[512,768]{1,0:T(8,128)(2,1)S(1)}, bf16[512,768]{1,0:T(8,128)(2,1)S(1)}, u32[]{:S(2)}, u32[]{:S(2)}) collective-permute-start(bf16[512,768]{1,0:T(8,128)(2,1)S(1)} %add_convert_fusion.1), channel_id=1, source_target_pairs={{8,0},{10,2},{12,4},{14,6},{16,8},{18,10},{20,12},{22,14},{24,16},... | collective-permute-start | bytes 2359304 | tf_op jit(solution)/shard_map/ppermute | solution.py:329
  767.7 25.2 %collective-permute-start.12 = (bf16[2,128,2048]{2,1,0:T(8,128)(2,1)}, bf16[2,128,2048]{2,1,0:T(8,128)(2,1)}, u32[]{:S(2)}, u32[]{:S(2)}) collective-permute-start(bf16[2,128,2048]{2,1,0:T(8,128)(2,1)} %slice.235), channel_id=1, source_target_pairs={{0,2},{2,0},{4,6},{6,4},{8,10},{10,8},{12,14},{14,12},{16,18},{18,... | collective-permute-start | bytes 3145736 | tf_op jit(solution)/shard_map/ppermute | solution.py:318
  768.5 25.9 %collective-permute-start.14 = (bf16[2,128,2048]{2,1,0:T(8,128)(2,1)}, bf16[2,128,2048]{2,1,0:T(8,128)(2,1)S(1)}, u32[]{:S(2)}, u32[]{:S(2)}) collective-permute-start(bf16[2,128,2048]{2,1,0:T(8,128)(2,1)} %slice.301), channel_id=1, source_target_pairs={{0,4},{2,6},{4,0},{6,2},{8,12},{10,14},{12,8},{14,10},{16,20},{18,... | collective-permute-start | bytes 3145736 | tf_op jit(solution)/shard_map/ppermute | solution.py:318
  770.8 49.4 %collective-permute-start.27 = (f32[2,128]{1,0:T(2,128)}, f32[2,128]{1,0:T(2,128)}, u32[]{:S(2)}, u32[]{:S(2)}) collective-permute-start(f32[2,128]{1,0:T(2,128)} %pad_maximum_fusion.2), channel_id=1, source_target_pairs={{0,1},{1,0},{2,3},{3,2},{4,5},{5,4},{6,7},{7,6},{8,9},{9,8},{10,11... | collective-permute-start | bytes 3080 | tf_op jit(solution)/shard_map/ppermute | solution.py:321
  796.5 12.9 %collective-permute-start.13 = (bf16[128,2048]{1,0:T(8,128)(2,1)S(1)}, bf16[128,2048]{1,0:T(8,128)(2,1)S(1)}, u32[]{:S(2)}, u32[]{:S(2)}) collective-permute-start(bf16[128,2048]{1,0:T(8,128)(2,1)S(1)} %get-tuple-element.144), channel_id=1, source_target_pairs={{0,4},{2,6},{4,0},{6,2},{8,12},{10,14},{12,8},{14,10},{16,20},{18,... | collective-permute-start | bytes 1572872 | tf_op jit(solution)/shard_map/ppermute | solution.py:318
  796.9 12.6 %collective-permute-start.15 = (bf16[128,2048]{1,0:T(8,128)(2,1)S(1)}, bf16[128,2048]{1,0:T(8,128)(2,1)S(1)}, u32[]{:S(2)}, u32[]{:S(2)}) collective-permute-start(bf16[128,2048]{1,0:T(8,128)(2,1)S(1)} %get-tuple-element.145), channel_id=1, source_target_pairs={{0,2},{2,0},{4,6},{6,4},{8,10},{10,8},{12,14},{14,12},{16,18},{18,... | collective-permute-start | bytes 1572872 | tf_op jit(solution)/shard_map/ppermute | solution.py:318
  798.7 13.0 %copy-start.31 = (f32[256,2048]{1,0:T(8,128)S(1)}, f32[256,2048]{1,0:T(8,128)}, u32[]{:S(2)}) copy-start(f32[256,2048]{1,0:T(8,128)} %get-tuple-element.59.resid_ref) | copy-start | bytes 6291460
  813.0 8.4 %collective-permute-start.16 = (bf16[256,2048]{1,0:T(8,128)(2,1)}, bf16[256,2048]{1,0:T(8,128)(2,1)}, u32[]{:S(2)}, u32[]{:S(2)}) collective-permute-start(bf16[256,2048]{1,0:T(8,128)(2,1)} %fusion.8), channel_id=1, source_target_pairs={{0,1},{1,0},{2,3},{3,2},{4,5},{5,4},{6,7},{7,6},{8,9},{9,8},{10,11... | collective-permute-start | bytes 3145736 | tf_op jit(solution)/shard_map/ppermute | solution.py:321
  (51 other events, 217.8 us)
